TPU v7x, 32 devices: a whole 2x2x4 slice. The times are simulated.
32 devices in a mesh: groups: 2 (over y), expert: 8 (over z, core), tensor: 2 (over x), dp: 1.
Axes of the slice: x: 2, y: 2, z: 4, core: 2. Of those that a mesh axis runs over, the one named last changes fastest.
Arguments:
- tokens: bfloat16 [2, 512, 4096], P(None, ('groups', 'expert', 'dp'), 'tensor'), parts along dimension 1, may hold values from -6 to 6
- expert_ids: int32 [2, 512, 16], P(None, ('groups', 'expert', 'dp')), parts along dimension 1, may hold values from 0 to 31, all different within a row; in each aligned block of 32 rows (0 to 31, 32 to 63, ..., all dimensions but the last counted through in order) at most 32 rows name the same one
- route_weights: int32 [2, 512, 16], P(None, ('groups', 'expert', 'dp')), parts along dimension 1, may hold values from 1 to 255
- expert_slot: int32 [32], replicated, may hold values from 0 to 31, each once
- latent_down: bfloat16 [4096, 1024], P('tensor'), may hold values from -0.09375 to 0.09375
- gate_proj: bfloat16 [32, 1024, 1024], P('expert', None, 'tensor'), may hold values from -0.1875 to 0.1875
- up_proj: bfloat16 [32, 1024, 1024], P('expert', None, 'tensor'), may hold values from -0.1875 to 0.1875
- down_proj: bfloat16 [32, 1024, 1024], P('expert', 'tensor'), may hold values from -0.1875 to 0.1875
- latent_up: bfloat16 [1024, 4096], P('tensor'), may hold values from -1.5 to 1.5
Outputs:
- layer_out: bfloat16 [2, 512, 4096], P(None, ('groups', 'expert', 'dp'), 'tensor'), parts along dimension 1
There are 2 independent parts, one for each index of `groups`. A program takes and returns all parts, laid end to end along the dimension named above; an argument that names none is the same for every part. Nothing has to cross between parts.
Inputs may be any that keep to these rules, and one draw needn't show every extreme that they name: `expert_ids`: each row names 16 different experts. In each aligned block of 32 rows (the rows of one device in one batch) no expert is named by more than 32 rows, and in some block one expert is named by exactly 32 rows. `expert_slot`: A permutation: every slot serves exactly one expert.
All inputs are finite; a program needn't handle non-finite values.
Results may differ from a plain program's by a relative error of at most 0.029.
Values may be sent and summed in bfloat16 or wider, within the bound.
No kernel may reach another device: no remote copies, remote signals or barrier semaphores. Data moves between devices by JAX's collectives and lax.ppermute only.
A program may use at most 64 MiB of HBM per device.

v0:
```python
import jax
import jax.numpy as jnp
from jax import lax
from jax.sharding import PartitionSpec as P


def weighted_sums(values, route_meta, row_count):
    peer_count = values.shape[0]
    flat_vals = values.reshape(peer_count, -1, values.shape[3]).astype(jnp.float32)
    gate_vals = route_meta[:, 1].astype(jnp.float32) / route_meta[:, 2].astype(jnp.float32)
    selector = (
        route_meta[:, 0][:, None, :] == jnp.arange(row_count, dtype=jnp.int32)[None, :, None]
    ).astype(jnp.float32)
    selector = selector * gate_vals[:, None, :]
    summed = jnp.einsum("prq,pqw->prw", selector, flat_vals, precision=lax.Precision.HIGHEST)
    return summed.astype(jnp.bfloat16)


def decode_batch(
    inputs, chosen, weights, expert_slot, latent_down, gate_proj, up_proj, down_proj, latent_up
):
    row_count = inputs.shape[0]
    top_count = chosen.shape[1]
    expert_count = expert_slot.shape[0]
    local_count = gate_proj.shape[0]
    peer_count = expert_count // local_count
    capacity = min(row_count, max(2 * row_count * top_count // expert_count, 2))
    pair_count = row_count * top_count
    slot_width = local_count * capacity
    tensor_count = lax.axis_size("tensor")
    lookup = (
        chosen[:, :, None] == jnp.arange(expert_count, dtype=jnp.int32)[None, None, :]
    ).astype(jnp.int32)
    slot_ids = jnp.sum(lookup * expert_slot[None, None, :], axis=2).reshape(pair_count)
    onehot = (slot_ids[:, None] == jnp.arange(expert_count, dtype=jnp.int32)[None, :]).astype(
        jnp.int32
    )
    position = jnp.sum(onehot * (jnp.cumsum(onehot, axis=0) - 1), axis=1)
    target = slot_ids * capacity + position
    source = (
        jnp.full((expert_count * capacity,), -1, jnp.int32)
        .at[target]
        .set(jnp.arange(pair_count, dtype=jnp.int32))
    )
    filled = source >= 0
    safe_ids = jnp.where(filled, source, 0)
    row_ids = jnp.where(filled, safe_ids // top_count, -1)
    totals = jnp.repeat(jnp.sum(weights, axis=1), top_count)
    weight_ids = jnp.where(filled, weights.reshape(pair_count)[safe_ids], 0)
    total_ids = jnp.where(filled, totals[safe_ids], 1)
    route_meta = jnp.stack(
        [
            row_ids.reshape(peer_count, slot_width),
            weight_ids.reshape(peer_count, slot_width),
            total_ids.reshape(peer_count, slot_width),
        ],
        axis=1,
    )
    take_rows = jnp.where(filled, safe_ids // top_count, 0)
    partial_latent = jnp.dot(inputs, latent_down, preferred_element_type=jnp.float32)
    latent = lax.psum(partial_latent.astype(jnp.bfloat16), "tensor")
    payload = jnp.where(filled[:, None], latent[take_rows], jnp.zeros((), jnp.bfloat16)).reshape(
        peer_count, slot_width, -1
    )
    arrived, meta_in = (
        lax.all_to_all(payload, "expert", split_axis=0, concat_axis=0, tiled=True),
        lax.all_to_all(route_meta, "expert", split_axis=0, concat_axis=0, tiled=True),
    )
    arrived = arrived.reshape(peer_count, local_count, capacity, -1)
    gate_act = jnp.einsum("sjcl,jlh->sjch", arrived, gate_proj, preferred_element_type=jnp.float32)
    up_act = jnp.einsum("sjcl,jlh->sjch", arrived, up_proj, preferred_element_type=jnp.float32)
    hidden = (jax.nn.silu(gate_act) * up_act).astype(jnp.bfloat16)
    partial_out = jnp.einsum(
        "sjch,jhl->sjcl", hidden, down_proj, preferred_element_type=jnp.float32
    )
    latent_width = partial_out.shape[3]
    block_width = latent_width // tensor_count
    rounded = partial_out.astype(jnp.bfloat16).reshape(
        peer_count, local_count, capacity, tensor_count, block_width
    )
    received = lax.all_to_all(rounded, "tensor", split_axis=3, concat_axis=3, tiled=True)
    expert_out = jnp.sum(received.astype(jnp.float32), axis=3).astype(jnp.bfloat16)
    returned = lax.all_to_all(expert_out, "expert", split_axis=0, concat_axis=0, tiled=True)
    shares = weighted_sums(returned, route_meta, row_count)
    mixed_rows = jnp.sum(shares.astype(jnp.float32), axis=0).astype(jnp.bfloat16)
    projected = jnp.dot(mixed_rows, latent_up, preferred_element_type=jnp.float32)
    summed = lax.psum_scatter(
        projected.astype(jnp.bfloat16), "tensor", scatter_dimension=1, tiled=True
    ).astype(jnp.float32)
    return (inputs.astype(jnp.float32) + summed).astype(jnp.bfloat16)


def shards(
    tokens,
    expert_ids,
    route_weights,
    expert_slot,
    latent_down,
    gate_proj,
    up_proj,
    down_proj,
    latent_up,
):
    results = []
    for step_index in range(tokens.shape[0]):
        results.append(
            decode_batch(
                tokens[step_index],
                expert_ids[step_index],
                route_weights[step_index],
                expert_slot,
                latent_down,
                gate_proj,
                up_proj,
                down_proj,
                latent_up,
            )
        )
    return jnp.stack(results)


def solution(mesh):
    in_specs = (
        P(None, ("groups", "expert", "dp"), "tensor"),
        P(None, ("groups", "expert", "dp"), None),
        P(None, ("groups", "expert", "dp"), None),
        P(),
        P("tensor", None),
        P("expert", None, "tensor"),
        P("expert", None, "tensor"),
        P("expert", "tensor", None),
        P("tensor", None),
    )
    out_specs = P(None, ("groups", "expert", "dp"), "tensor")
    return jax.shard_map(shards, mesh=mesh, in_specs=in_specs, out_specs=out_specs, check_vma=False)
```

profile of v0, /device:TPU:0, one launch (start us, length us, event | category | flops | bytes accessed | tf_op | source)
XLA Modules:
  0.0 310.7 jit_solution(14592452509656133563)
XLA Ops:
  6.5 3.9 %convolution_convert_fusion.4 = bf16[32,1024]{1,0:T(8,128)(2,1)} fusion(bf16[2048,1024]{1,0:T(8,128)(2,1)} %param.13, bf16[2,32,2048]{2,1,0:T(8,128)(2,1)} %param.9), kind=kOutput, calls=%fused_computation.50 | convolution fusion | flops 134250496 | bytes 4390912 | tf_op jit(solution)/shard_map/dot_general | solution.py:60
  18.6 18.6 %all-reduce.3.cloned.1.call-done = (bf16[32,1024]{1,0:T(8,128)(2,1)}, bf16[32,1024]{1,0:T(8,128)(2,1)}) async-done(((bf16[32,1024]{1,0:T(8,128)(2,1)}, bf16[32,1024]{1,0:T(8,128)(2,1)}), (bf16[32,1024]{1,0:T(8,128)(2,1)}, bf16[32,1024]{1,0:T(8,128)(2,1)})) %all-reduce.3.cloned.1.call-update) | async-done | bytes 131088 | tf_op jit(solution)/shard_map/psum | solution.py:61
  37.2 5.8 %gather_fusion.5 = bf16[1024,1024]{1,0:T(8,128)(2,1)S(1)} fusion(bf16[32,1024]{1,0:T(8,128)(2,1)} %get-tuple-element.9, s32[1024]{0:T(1024)S(1)} %get-tuple-element.21), kind=kCustom, calls=%fused_computation.5 | custom fusion | bytes 4198400 | tf_op jit(solution)/shard_map/gather | solution.py:62
  44.6 4.7 %all-to-all-start.3 = ((bf16[8,128,1024]{2,1,0:T(8,128)(2,1)}), bf16[8,128,1024]{2,1,0:T(8,128)(2,1)}, u32[]{:S(2)}, u32[]{:S(2)}) async-start(bf16[8,128,1024]{2,1,0:T(8,128)(2,1)} %broadcast_select_fusion), calls=%async_computation.4 | async-start | bytes 4194304 | tf_op jit(solution)/shard_map/all_to_all | solution.py:66
  53.7 4.1 %gather_fusion.2 = bf16[1024,1024]{1,0:T(8,128)(2,1)S(1)} fusion(bf16[32,1024]{1,0:T(8,128)(2,1)S(1)} %copy-done, s32[1024]{0:T(1024)S(1)} %get-tuple-element.18), kind=kCustom, calls=%fused_computation.2 | custom fusion | bytes 4198400 | tf_op jit(solution)/shard_map/gather | solution.py:62
  59.3 39.3 %all-to-all-done.3 = bf16[8,128,1024]{2,1,0:T(8,128)(2,1)} async-done(((bf16[8,128,1024]{2,1,0:T(8,128)(2,1)}), bf16[8,128,1024]{2,1,0:T(8,128)(2,1)}, u32[]{:S(2)}, u32[]{:S(2)}) %all-to-all-start.3) | async-done | bytes 2097184 | tf_op jit(solution)/shard_map/all_to_all | solution.py:66
  102.2 5.4 %fusion.4 = f32[4,8,32,512]{3,2,1,0:T(8,128)} fusion(bf16[4,1024,512]{2,1,0:T(8,128)(2,1)} %param.15, bf16[8,4,32,1024]{3,2,1,0:T(8,128)(2,1)} %bitcast.30), kind=kOutput, calls=%fused_computation.14 | convolution fusion | flops 1073741824 | bytes 8388608 | tf_op jit(solution)/shard_map/sjcl,jlh->sjch/dot_general | solution.py:71
  107.6 8.4 %fusion.23 = bf16[4,8,32,1024]{3,2,1,0:T(8,128)(2,1)} fusion(bf16[4,512,1024]{2,1,0:T(8,128)(2,1)} %param.16, f32[4,8,32,512]{3,2,1,0:T(8,128)} %fusion.4, bf16[4,1024,512]{2,1,0:T(8,128)(2,1)} %param.14, bf16[8,4,32,1024]{3,2,1,0:T(8,128)(2,1)} %bitcast.30), kind=kOutput, calls=%fused_computation.41 | convolution fusion | flops 2151677952 | bytes 14680064 | tf_op jit(solution)/shard_map/sjch,jhl->sjcl/dot_general | solution.py:73
  119.2 31.9 %all-to-all-done = bf16[8,128,1024]{2,1,0:T(8,128)(2,1)S(1)} async-done(((bf16[8,128,1024]{2,1,0:T(8,128)(2,1)}), bf16[8,128,1024]{2,1,0:T(8,128)(2,1)S(1)}, u32[]{:S(2)}, u32[]{:S(2)}) %all-to-all-start) | async-done | bytes 2097184 | tf_op jit(solution)/shard_map/all_to_all | solution.py:66
  152.4 3.9 %all-to-all-start.4 = ((bf16[8,4,32,2,512]{4,2,0,1,3:T(8,128)(2,1)}), bf16[8,4,32,2,512]{4,2,0,1,3:T(8,128)(2,1)S(1)}, u32[]{:S(2)}, u32[]{:S(2)}) async-start(bf16[8,4,32,2,512]{4,2,0,1,3:T(8,128)(2,1)} %bitcast.159), calls=%async_computation.5 | async-start | bytes 4194304 | tf_op jit(solution)/shard_map/all_to_all | solution.py:81
  156.4 5.4 %fusion.6 = f32[4,8,32,512]{3,2,1,0:T(8,128)} fusion(bf16[4,1024,512]{2,1,0:T(8,128)(2,1)} %param.15, bf16[8,4,32,1024]{3,2,1,0:T(8,128)(2,1)} %bitcast.161), kind=kOutput, calls=%fused_computation.16 | convolution fusion | flops 1073741824 | bytes 8388608 | tf_op jit(solution)/shard_map/sjcl,jlh->sjch/dot_general | solution.py:71
  161.8 8.4 %fusion.20 = bf16[4,8,32,1024]{3,2,1,0:T(8,128)(2,1)} fusion(bf16[4,512,1024]{2,1,0:T(8,128)(2,1)} %param.16, f32[4,8,32,512]{3,2,1,0:T(8,128)} %fusion.6, bf16[4,1024,512]{2,1,0:T(8,128)(2,1)} %param.14, bf16[8,4,32,1024]{3,2,1,0:T(8,128)(2,1)} %bitcast.162), kind=kOutput, calls=%fused_computation.40 | convolution fusion | flops 2151677952 | bytes 14680064 | tf_op jit(solution)/shard_map/sjch,jhl->sjcl/dot_general | solution.py:73
  173.4 7.7 %all-to-all-done.4 = bf16[8,4,32,2,512]{4,2,0,1,3:T(8,128)(2,1)S(1)} async-done(((bf16[8,4,32,2,512]{4,2,0,1,3:T(8,128)(2,1)}), bf16[8,4,32,2,512]{4,2,0,1,3:T(8,128)(2,1)S(1)}, u32[]{:S(2)}, u32[]{:S(2)}) %all-to-all-start.4) | async-done | bytes 2097184 | tf_op jit(solution)/shard_map/all_to_all | solution.py:81
  181.1 4.8 %all-to-all-start.1 = ((bf16[8,4,32,2,512]{4,2,0,1,3:T(8,128)(2,1)}), bf16[8,4,32,2,512]{4,2,0,1,3:T(8,128)(2,1)}, u32[]{:S(2)}, u32[]{:S(2)}) async-start(bf16[8,4,32,2,512]{4,2,0,1,3:T(8,128)(2,1)} %bitcast.160), calls=%async_computation.1 | async-start | bytes 4194304 | tf_op jit(solution)/shard_map/all_to_all | solution.py:81
  187.6 22.4 %all-to-all-done.1 = bf16[8,4,32,2,512]{4,2,0,1,3:T(8,128)(2,1)} async-done(((bf16[8,4,32,2,512]{4,2,0,1,3:T(8,128)(2,1)}), bf16[8,4,32,2,512]{4,2,0,1,3:T(8,128)(2,1)}, u32[]{:S(2)}, u32[]{:S(2)}) %all-to-all-start.1) | async-done | bytes 2097184 | tf_op jit(solution)/shard_map/all_to_all | solution.py:81
  216.8 23.3 %all-to-all-done.5 = bf16[8,4,32,512]{3,2,1,0:T(8,128)(2,1)S(1)} async-done(((bf16[8,4,32,512]{3,2,1,0:T(8,128)(2,1)}), bf16[8,4,32,512]{3,2,1,0:T(8,128)(2,1)S(1)}, u32[]{:S(2)}, u32[]{:S(2)}) %all-to-all-start.5) | async-done | bytes 1048608 | tf_op jit(solution)/shard_map/all_to_all | solution.py:83
  244.1 6.9 %gather_fusion.3 = s32[1024]{0:T(1024)S(1)} fusion(s32[512]{0:T(512)S(1)} %reshape_squeeze.7, s32[1024]{0:T(1024)S(1)} %get-tuple-element.22), kind=kCustom, calls=%fused_computation.3 | custom fusion | bytes 12288 | tf_op jit(solution)/shard_map/gather | solution.py:49
  250.9 6.9 %gather_fusion.4 = s32[1024]{0:T(1024)S(1)} fusion(s32[512]{0:T(512)S(1)} %reshape.175, s32[1024]{0:T(1024)S(1)} %get-tuple-element.22), kind=kCustom, calls=%fused_computation.4 | custom fusion | bytes 12288 | tf_op jit(solution)/shard_map/gather | solution.py:50
  258.1 6.9 %gather_fusion = s32[1024]{0:T(1024)S(1)} fusion(s32[512]{0:T(512)S(1)} %reshape_squeeze.6, s32[1024]{0:T(1024)S(1)} %get-tuple-element.19), kind=kCustom, calls=%fused_computation | custom fusion | bytes 12288 | tf_op jit(solution)/shard_map/gather | solution.py:49
  265.0 6.9 %gather_fusion.1 = s32[1024]{0:T(1024)S(1)} fusion(s32[512]{0:T(512)S(1)} %reshape.170, s32[1024]{0:T(1024)S(1)} %get-tuple-element.19), kind=kCustom, calls=%fused_computation.1 | custom fusion | bytes 12288 | tf_op jit(solution)/shard_map/gather | solution.py:50
  272.4 3.7 %convolution_convert_fusion = bf16[32,4096]{1,0:T(8,128)(2,1)} fusion(bf16[32,512]{1,0:T(8,128)(2,1)S(1)} %fusion.31, bf16[512,4096]{1,0:T(8,128)(2,1)} %param.17), kind=kOutput, calls=%fused_computation.8 | convolution fusion | flops 134348800 | bytes 4489216 | tf_op jit(solution)/shard_map/dot_general | solution.py:86
  276.8 3.8 %convolution_convert_fusion.1 = bf16[32,4096]{1,0:T(8,128)(2,1)} fusion(bf16[32,512]{1,0:T(8,128)(2,1)S(1)} %fusion.30, bf16[512,4096]{1,0:T(8,128)(2,1)} %param.17), kind=kOutput, calls=%fused_computation.9 | convolution fusion | flops 134348800 | bytes 4489216 | tf_op jit(solution)/shard_map/dot_general | solution.py:86
  280.6 7.8 %reduce-scatter.5.cloned.1.call-done = bf16[32,2048]{1,0:T(8,128)(2,1)} async-done(((bf16[32,4096]{1,0:T(8,128)(2,1)}), bf16[32,2048]{1,0:T(8,128)(2,1)}) %reduce-scatter.5.cloned.1.call-update) | async-done | bytes 131088 | tf_op jit(solution)/shard_map/reduce_scatter | solution.py:87
  288.4 14.0 %reduce-scatter.3.cloned.1.call-done = bf16[32,2048]{1,0:T(8,128)(2,1)} async-done(((bf16[32,4096]{1,0:T(8,128)(2,1)}), bf16[32,2048]{1,0:T(8,128)(2,1)}) %reduce-scatter.3.cloned.1.call-update) | async-done | bytes 131088 | tf_op jit(solution)/shard_map/reduce_scatter | solution.py:87
  (83 shorter events, 42.4 us)
Async XLA Ops:
  6.5 30.7 %all-reduce.3.cloned.1.call-start = ((), (), s32[]{:S(2)}) async-start(), calls=%async_computation.10 | async-start | bytes 262144 | tf_op jit(solution)/shard_map/psum | solution.py:61
  6.5 3.9 %copy-start.1 = (bf16[2048,1024]{1,0:T(8,128)(2,1)S(1)}, bf16[2048,1024]{1,0:T(8,128)(2,1)}, u32[]{:S(2)}) copy-start(bf16[2048,1024]{1,0:T(8,128)(2,1)} %param.13) | copy-start | bytes 12582916
  10.4 2.4 copy-start.4
  10.4 2.6 copy-start.6
  44.6 9.1 %copy-start = (bf16[32,1024]{1,0:T(8,128)(2,1)S(1)}, bf16[32,1024]{1,0:T(8,128)(2,1)}, u32[]{:S(2)}) copy-start(bf16[32,1024]{1,0:T(8,128)(2,1)} %get-tuple-element.10) | copy-start | bytes 196612
  44.6 53.9 %all-to-all-start.3 = ((bf16[8,128,1024]{2,1,0:T(8,128)(2,1)}), bf16[8,128,1024]{2,1,0:T(8,128)(2,1)}, u32[]{:S(2)}, u32[]{:S(2)}) async-start(bf16[8,128,1024]{2,1,0:T(8,128)(2,1)} %broadcast_select_fusion), calls=%async_computation.4 | async-start | bytes 4194304 | tf_op jit(solution)/shard_map/all_to_all | solution.py:66
  98.5 52.6 %all-to-all-start = ((bf16[8,128,1024]{2,1,0:T(8,128)(2,1)}), bf16[8,128,1024]{2,1,0:T(8,128)(2,1)S(1)}, u32[]{:S(2)}, u32[]{:S(2)}) async-start(bf16[8,128,1024]{2,1,0:T(8,128)(2,1)} %broadcast_select_fusion.1), calls=%async_computation | async-start | bytes 4194304 | tf_op jit(solution)/shard_map/all_to_all | solution.py:66
  151.1 1.3 copy-start.2
  152.4 28.7 %all-to-all-start.4 = ((bf16[8,4,32,2,512]{4,2,0,1,3:T(8,128)(2,1)}), bf16[8,4,32,2,512]{4,2,0,1,3:T(8,128)(2,1)S(1)}, u32[]{:S(2)}, u32[]{:S(2)}) async-start(bf16[8,4,32,2,512]{4,2,0,1,3:T(8,128)(2,1)} %bitcast.159), calls=%async_computation.5 | async-start | bytes 4194304 | tf_op jit(solution)/shard_map/all_to_all | solution.py:81
  181.1 28.9 %all-to-all-start.1 = ((bf16[8,4,32,2,512]{4,2,0,1,3:T(8,128)(2,1)}), bf16[8,4,32,2,512]{4,2,0,1,3:T(8,128)(2,1)}, u32[]{:S(2)}, u32[]{:S(2)}) async-start(bf16[8,4,32,2,512]{4,2,0,1,3:T(8,128)(2,1)} %bitcast.160), calls=%async_computation.1 | async-start | bytes 4194304 | tf_op jit(solution)/shard_map/all_to_all | solution.py:81
  210.0 30.1 %all-to-all-start.5 = ((bf16[8,4,32,512]{3,2,1,0:T(8,128)(2,1)}), bf16[8,4,32,512]{3,2,1,0:T(8,128)(2,1)S(1)}, u32[]{:S(2)}, u32[]{:S(2)}) async-start(bf16[8,4,32,512]{3,2,1,0:T(8,128)(2,1)} %copy.67), calls=%async_computation.6 | async-start | bytes 2097152 | tf_op jit(solution)/shard_map/all_to_all | solution.py:83
  215.7 28.0 %copy-start.5 = (s32[2,32,16]{1,2,0:T(8,128)S(1)}, s32[2,32,16]{1,2,0:T(8,128)}, u32[]{:S(2)}) copy-start(s32[2,32,16]{1,2,0:T(8,128)} %param.11) | copy-start | bytes 12292
  240.1 36.2 %all-to-all-start.2 = ((bf16[8,4,32,512]{3,2,1,0:T(8,128)(2,1)}), bf16[8,4,32,512]{3,2,1,0:T(8,128)(2,1)S(1)}, u32[]{:S(2)}, u32[]{:S(2)}) async-start(bf16[8,4,32,512]{3,2,1,0:T(8,128)(2,1)} %copy.59), calls=%async_computation.2 | async-start | bytes 2097152 | tf_op jit(solution)/shard_map/all_to_all | solution.py:83
  243.7 44.7 %reduce-scatter.5.cloned.1.call-start = ((), (), s32[]{:S(2)}) async-start(), calls=%async_computation.9 | async-start | bytes 393216 | tf_op jit(solution)/shard_map/reduce_scatter | solution.py:87
  276.2 26.2 %reduce-scatter.3.cloned.1.call-start = ((), (), s32[]{:S(2)}) async-start(), calls=%async_computation.8 | async-start | bytes 393216 | tf_op jit(solution)/shard_map/reduce_scatter | solution.py:87
  276.8 25.6 %copy-start.3 = (bf16[2,32,2048]{2,1,0:T(8,128)(2,1)S(1)}, bf16[2,32,2048]{2,1,0:T(8,128)(2,1)}, u32[]{:S(2)}) copy-start(bf16[2,32,2048]{2,1,0:T(8,128)(2,1)} %param.9) | copy-start | bytes 786436
  303.4 0.7 copy-start.7
Sparse Core Ops, SparseCore 0:
  12.9 24.2 all-reduce.2
  276.3 12.0 reduce-scatter.4
  290.7 11.6 reduce-scatter.2
where the time goes:
time: 311 us
  waiting for transfers between devices  165 us (53%)
  local copies, waits for them, and re-layouts  54.5 us (18%)
  matrix products  42.4 us (14%)
  starting transfers between devices  24.3 us (8%)
  between operations  13.4 us (4%)
  other arithmetic  10.9 us (4%)
    all_to_all x2, waiting for transfers between devices, decode_batch(): lax.all_to_all(payload, 'expert', split_axis=0, concat_axis=0, tiled=True)  71.2 us
    all_to_all x2, waiting for transfers between devices, decode_batch(): lax.all_to_all(rounded, 'tensor', split_axis=3, concat_axis=3, tiled=True)  30.1 us
    all_to_all x2, waiting for transfers between devices, decode_batch(): lax.all_to_all(expert_out, 'expert', split_axis=0, concat_axis=0, tiled=T...  23.3 us
    reduce_scatter x2, waiting for transfers between devices, decode_batch(): lax.psum_scatter(projected.astype(jnp.bfloat16), 'tensor', scatter_dimens...  21.8 us
    psum x1, waiting for transfers between devices, decode_batch(): latent = lax.psum(partial_latent.astype(jnp.bfloat16), 'tensor')  18.6 us
    dot_general x2, matrix products, decode_batch(): jnp.einsum('sjch,jhl->sjcl', hidden, down_proj, preferred_element_type=jn...  16.8 us
    gather x2, local copies, waits for them, and re-layouts, decode_batch(): weight_ids = jnp.where(filled, weights.reshape(pair_count)[safe_ids], 0)  13.7 us
    gather x2, local copies, waits for them, and re-layouts, decode_batch(): total_ids = jnp.where(filled, totals[safe_ids], 1)  13.7 us
  transfers between devices with their start and end apart: 9, of which 8 were waited for; matrix products, arithmetic and copies ran while one was open for 29% of the time, Pallas kernels for 0%

commit v1 on v0

v1 whole, which is shorter than its diff:
```python
import functools

import jax
import jax.numpy as jnp
from jax import lax
from jax.experimental import pallas as pl
from jax.experimental.pallas import tpu as pltpu
from jax.sharding import PartitionSpec as P

LANES = 128


def expert_kernel(rows_ref, weight_ref, gate_ref, up_ref, down_ref, out_ref, total_ref):
    step = pl.program_id(0)

    @pl.when(step == 0)
    def _():
        total_ref[...] = jnp.zeros_like(total_ref)

    rows = rows_ref[...]
    gate_act = jnp.dot(rows, gate_ref[0], preferred_element_type=jnp.float32)
    up_act = jnp.dot(rows, up_ref[0], preferred_element_type=jnp.float32)
    lanes = lax.broadcasted_iota(jnp.int32, weight_ref.shape, 1)
    weight = jnp.sum(
        jnp.where(lanes == step, weight_ref[...], 0.0), axis=1, keepdims=True
    )
    hidden = (gate_act / (1.0 + jnp.exp(-gate_act)) * up_act * weight).astype(jnp.bfloat16)
    total_ref[...] += jnp.dot(hidden, down_ref[0], preferred_element_type=jnp.float32)

    @pl.when(step == pl.num_programs(0) - 1)
    def _():
        out_ref[...] = total_ref[...].astype(out_ref.dtype)


def experts(rows, weights, gate_proj, up_proj, down_proj):
    row_count, width = rows.shape
    local_count, _, hidden = gate_proj.shape
    return pl.pallas_call(
        expert_kernel,
        grid=(local_count,),
        in_specs=[
            pl.BlockSpec((row_count, width), lambda j: (0, 0)),
            pl.BlockSpec((row_count, LANES), lambda j: (0, 0)),
            pl.BlockSpec((1, width, hidden), lambda j: (j, 0, 0)),
            pl.BlockSpec((1, width, hidden), lambda j: (j, 0, 0)),
            pl.BlockSpec((1, hidden, width), lambda j: (j, 0, 0)),
        ],
        out_specs=pl.BlockSpec((row_count, width), lambda j: (0, 0)),
        out_shape=jax.ShapeDtypeStruct((row_count, width), jnp.bfloat16),
        scratch_shapes=[pltpu.VMEM((row_count, width), jnp.float32)],
        compiler_params=pltpu.CompilerParams(vmem_limit_bytes=40 * 1024 * 1024),
    )(rows, weights, gate_proj, up_proj, down_proj)


def shift(x, axis, size, by):
    return lax.ppermute(x, axis, [(i, (i + by) % size) for i in range(size)])


def add(*terms):
    return functools.reduce(jnp.add, [t.astype(jnp.float32) for t in terms])


def slot_weights(expert_ids, route_weights, expert_slot):
    expert_count = expert_slot.shape[0]
    every = jnp.arange(expert_count, dtype=jnp.int32)
    chosen = expert_ids[:, :, None] == every[None, None, :]
    by_expert = jnp.sum(jnp.where(chosen, route_weights[:, :, None], 0), axis=1)
    move = expert_slot[:, None] == every[None, :]
    by_slot = jnp.dot(
        by_expert.astype(jnp.bfloat16), move.astype(jnp.bfloat16), preferred_element_type=jnp.float32
    )
    return by_slot.astype(jnp.bfloat16)


def shards(
    tokens,
    expert_ids,
    route_weights,
    expert_slot,
    latent_down,
    gate_proj,
    up_proj,
    down_proj,
    latent_up,
):
    steps, step_rows, features = tokens.shape
    rows = steps * step_rows
    latent_width = latent_down.shape[1]
    local_count = gate_proj.shape[0]
    tensor_count = lax.axis_size("tensor")
    expert_axis = lax.axis_size("expert")
    pair = 2 if expert_axis % 2 == 0 else 1
    far = expert_axis // pair
    tensor_index = lax.axis_index("tensor")
    expert_index = lax.axis_index("expert")

    def swap(x):
        return lax.ppermute(x, "expert", [(i, i ^ 1) for i in range(expert_axis)])

    inputs = tokens.reshape(rows, features)
    ids = expert_ids.reshape(rows, -1)
    route = route_weights.reshape(rows, -1)

    partial = jnp.dot(inputs, latent_down, preferred_element_type=jnp.float32).astype(jnp.bfloat16)
    latent = add(
        partial, *[shift(partial, "tensor", tensor_count, s) for s in range(1, tensor_count)]
    ).astype(jnp.bfloat16)

    weights = slot_weights(ids, route, expert_slot)
    slots = weights.shape[1]
    padded = -(-slots // LANES) * LANES
    payload = jnp.concatenate([latent, jnp.pad(weights, ((0, 0), (0, padded - slots)))], axis=1)

    near = jnp.concatenate(
        [payload] + [shift(payload, "expert", expert_axis, s * pair) for s in range(1, far)], axis=0
    )
    gathered = jnp.concatenate([near, swap(near)], axis=0) if pair == 2 else near
    mine = lax.dynamic_slice_in_dim(
        gathered[:, latent_width:], expert_index * local_count, local_count, axis=1
    ).astype(jnp.float32)
    mine = jnp.pad(mine, ((0, 0), (0, LANES - local_count)))
    mixed = experts(gathered[:, :latent_width], mine, gate_proj, up_proj, down_proj)

    if pair == 2:
        half = far * rows
        mixed = add(mixed[:half], swap(mixed[half:])).astype(jnp.bfloat16)
    block = latent_width // tensor_count

    def features_of(x, index, width):
        return lax.dynamic_slice_in_dim(x, index * width, width, axis=1)

    own = features_of(mixed, tensor_index, block)
    for s in range(1, tensor_count):
        away = features_of(mixed, (tensor_index + s) % tensor_count, block)
        own = add(own, shift(away, "tensor", tensor_count, s))
    own = own.astype(jnp.bfloat16).reshape(far, rows, block)
    total = add(
        own[0], *[shift(own[s], "expert", expert_axis, -s * pair) for s in range(1, far)]
    )
    norm = jnp.sum(route, axis=1, keepdims=True).astype(jnp.float32)
    mixed_rows = (total / norm).astype(jnp.bfloat16)

    result = inputs.astype(jnp.float32)
    for s in range(1, tensor_count):
        away = jnp.dot(
            mixed_rows,
            features_of(latent_up, (tensor_index + s) % tensor_count, features),
            preferred_element_type=jnp.float32,
        ).astype(jnp.bfloat16)
        result = result + shift(away, "tensor", tensor_count, s).astype(jnp.float32)
    result = result + jnp.dot(
        mixed_rows, features_of(latent_up, tensor_index, features), preferred_element_type=jnp.float32
    )
    return result.astype(jnp.bfloat16).reshape(steps, step_rows, features)


def solution(mesh):
    in_specs = (
        P(None, ("groups", "expert", "dp"), "tensor"),
        P(None, ("groups", "expert", "dp"), None),
        P(None, ("groups", "expert", "dp"), None),
        P(),
        P("tensor", None),
        P("expert", None, "tensor"),
        P("expert", None, "tensor"),
        P("expert", "tensor", None),
        P("tensor", None),
    )
    out_specs = P(None, ("groups", "expert", "dp"), "tensor")
    return jax.shard_map(shards, mesh=mesh, in_specs=in_specs, out_specs=out_specs, check_vma=False)
```

time: 311 us -> 73 us (0.23)
  waiting for transfers between devices: 165 us -> 32.3 us
  local copies, waits for them, and re-layouts: 54.5 us -> 4.85 us
  matrix products: 42.4 us -> 8.31 us
  between operations: 13.4 us -> 0.19 us
  other arithmetic: 10.9 us -> 0.55 us
  Pallas kernels: 0 us -> 8.93 us
  starting transfers between devices: 24.3 us -> 17.6 us
    all_to_all x6 -> x0, waiting for transfers between devices: 125 us -> none  [the longest x2 71.2 us: decode_batch(): lax.all_to_all(payload, 'expert', split_axis=0, concat_axis=0, tiled=True)]
    gather x6 -> x0, local copies, waits for them, and re-layouts: 37.4 us -> none  [the longest x2 13.7 us: decode_batch(): weight_ids = jnp.where(filled, weights.reshape(pair_count)[safe_ids], 0)]
    dot_general x10 -> x4, matrix products: 42.4 us -> 8.31 us  [the longest x1 3.15 us: shards(): jnp.dot(inputs, latent_down, preferred_element_type=jnp.float32)]
    ppermute x0 -> x11, waiting for transfers between devices: none -> 32.3 us  [the longest x9 28.6 us: shift(): return lax.ppermute(x, axis, [(i, (i + by) % size) for i in range(size)])]
    all_to_all x6 -> x0, starting transfers between devices: 24.2 us -> none  [the longest x2 8.76 us: decode_batch(): lax.all_to_all(rounded, 'tensor', split_axis=3, concat_axis=3, tiled=True)]
    reduce_scatter x2 -> x0, waiting for transfers between devices: 21.8 us -> none  [decode_batch(): lax.psum_scatter(projected.astype(jnp.bfloat16), 'tensor', scatter_dimens...]
    psum x1 -> x0, waiting for transfers between devices: 18.6 us -> none  [decode_batch(): latent = lax.psum(partial_latent.astype(jnp.bfloat16), 'tensor')]
    ppermute x0 -> x11, starting transfers between devices: none -> 17.6 us  [the longest x9 17.3 us: shift(): return lax.ppermute(x, axis, [(i, (i + by) % size) for i in range(size)])]
  transfers between devices with their start and end apart: 9 -> 11, of which waited for: 8 -> 10; matrix products, arithmetic and copies ran while one was open for 29% -> 1% of each run, Pallas kernels for 0% -> 0%
where the time goes in v1:
time: 73 us; the launch traced here: 72.7 us
  waiting for transfers between devices  32.3 us (44%)
  starting transfers between devices  17.6 us (24%)
  Pallas kernels  8.93 us (12%)
  matrix products  8.31 us (11%)
  local copies, waits for them, and re-layouts  4.85 us (7%)
    ppermute x9, waiting for transfers between devices, shift(): return lax.ppermute(x, axis, [(i, (i + by) % size) for i in range(size)])  28.6 us
    ppermute x9, starting transfers between devices, shift(): return lax.ppermute(x, axis, [(i, (i + by) % size) for i in range(size)])  17.3 us
    pallas_call x1, Pallas kernels, experts(): pl.pallas_call(expert_kernel, grid=(local_count,), in_specs=[pl.BlockSpec...  8.93 us
    unnamed x17, local copies, waits for them, and re-layouts  4.09 us
    ppermute x2, waiting for transfers between devices, swap(): return lax.ppermute(x, 'expert', [(i, i ^ 1) for i in range(expert_axis)])  3.69 us
    dot_general x1, matrix products, shards(): jnp.dot(inputs, latent_down, preferred_element_type=jnp.float32)  3.15 us
    dot_general x1, matrix products, shards(): jnp.dot(mixed_rows, features_of(latent_up, tensor_index, features), prefe...  2.78 us
    dot_general x1, matrix products, shards(): jnp.dot(mixed_rows, features_of(latent_up, (tensor_index + s) % tensor_co...  2.12 us
  transfers between devices with their start and end apart: 11, of which 10 were waited for; matrix products, arithmetic and copies ran while one was open for 1% of the time, Pallas kernels for 0%

profile of v1, /device:TPU:0, one launch (start us, length us, event | category | flops | bytes accessed | tf_op | source)
XLA Modules:
  0.0 72.7 jit_solution(5031806705469164919)
XLA Ops:
  0.0 3.2 %convolution_convert_fusion.1 = bf16[64,1024]{1,0:T(8,128)(2,1)S(1)} fusion(bf16[64,2048]{1,0:T(8,128)(2,1)} %bitcast.10, bf16[2048,1024]{1,0:T(8,128)(2,1)} %param.13), kind=kOutput, calls=%fused_computation.4 | convolution fusion | flops 268500992 | bytes 4587520 | tf_op jit(solution)/shard_map/dot_general | solution.py:104
  3.2 3.0 %collective-permute-start = (bf16[64,1024]{1,0:T(8,128)(2,1)S(1)}, bf16[64,1024]{1,0:T(8,128)(2,1)S(1)}, u32[]{:S(2)}, u32[]{:S(2)}) collective-permute-start(bf16[64,1024]{1,0:T(8,128)(2,1)S(1)} %convolution_convert_fusion.1), channel_id=1, source_target_pairs={{0,1},{1,0},{2,3},{3,2},{4,5},{5,4},{6,7},{7,6},{8,9},{9,8},{10,11... | collective-permute-start | bytes 393224 | tf_op jit(solution)/shard_map/ppermute | solution.py:56
  6.8 2.9 %collective-permute-done = bf16[64,1024]{1,0:T(8,128)(2,1)S(1)} collective-permute-done((bf16[64,1024]{1,0:T(8,128)(2,1)S(1)}, bf16[64,1024]{1,0:T(8,128)(2,1)S(1)}, u32[]{:S(2)}, u32[]{:S(2)}) %collective-permute-start) | collective-permute-done | bytes 131104 | tf_op jit(solution)/shard_map/ppermute | solution.py:56
  9.7 1.9 %collective-permute-start.1 = (bf16[64,1152]{1,0:T(8,128)(2,1)S(1)}, bf16[64,1152]{1,0:T(8,128)(2,1)S(1)}, u32[]{:S(2)}, u32[]{:S(2)}) collective-permute-start(bf16[64,1152]{1,0:T(8,128)(2,1)S(1)} %get-tuple-element.8), channel_id=1, source_target_pairs={{0,4},{2,6},{4,8},{6,10},{8,12},{10,14},{12,0},{14,2},{1,5},{3,7},... | collective-permute-start | bytes 442376 | tf_op jit(solution)/shard_map/ppermute | solution.py:56
  11.6 2.6 %collective-permute-start.2 = (bf16[64,1152]{1,0:T(8,128)(2,1)S(1)}, bf16[64,1152]{1,0:T(8,128)(2,1)S(1)}, u32[]{:S(2)}, u32[]{:S(2)}) collective-permute-start(bf16[64,1152]{1,0:T(8,128)(2,1)S(1)} %get-tuple-element.8), channel_id=1, source_target_pairs={{0,8},{2,10},{4,12},{6,14},{8,0},{10,2},{12,4},{14,6},{1,9},{3,11}... | collective-permute-start | bytes 442376 | tf_op jit(solution)/shard_map/ppermute | solution.py:56
  14.2 1.3 %collective-permute-start.3 = (bf16[64,1152]{1,0:T(8,128)(2,1)S(1)}, bf16[64,1152]{1,0:T(8,128)(2,1)S(1)}, u32[]{:S(2)}, u32[]{:S(2)}) collective-permute-start(bf16[64,1152]{1,0:T(8,128)(2,1)S(1)} %get-tuple-element.8), channel_id=1, source_target_pairs={{0,12},{2,14},{4,0},{6,2},{8,4},{10,6},{12,8},{14,10},{1,13},{3,15... | collective-permute-start | bytes 442376 | tf_op jit(solution)/shard_map/ppermute | solution.py:56
  15.6 3.0 %collective-permute-done.1 = bf16[64,1152]{1,0:T(8,128)(2,1)S(1)} collective-permute-done((bf16[64,1152]{1,0:T(8,128)(2,1)S(1)}, bf16[64,1152]{1,0:T(8,128)(2,1)S(1)}, u32[]{:S(2)}, u32[]{:S(2)}) %collective-permute-start.1) | collective-permute-done | bytes 147488 | tf_op jit(solution)/shard_map/ppermute | solution.py:56
  18.6 4.5 %collective-permute-done.2 = bf16[64,1152]{1,0:T(8,128)(2,1)S(1)} collective-permute-done((bf16[64,1152]{1,0:T(8,128)(2,1)S(1)}, bf16[64,1152]{1,0:T(8,128)(2,1)S(1)}, u32[]{:S(2)}, u32[]{:S(2)}) %collective-permute-start.2) | collective-permute-done | bytes 147488 | tf_op jit(solution)/shard_map/ppermute | solution.py:56
  23.2 1.9 %collective-permute-done.4 = bf16[256,1152]{1,0:T(8,128)(2,1)S(1)} collective-permute-done((bf16[256,1152]{1,0:T(8,128)(2,1)S(1)}, bf16[256,1152]{1,0:T(8,128)(2,1)S(1)}, u32[]{:S(2)}, u32[]{:S(2)}) %collective-permute-start.4) | collective-permute-done | bytes 589856 | tf_op jit(solution)/shard_map/ppermute | solution.py:98
  25.5 1.8 %copy-done = bf16[4,1024,512]{2,1,0:T(8,128)(2,1)S(1)} copy-done((bf16[4,1024,512]{2,1,0:T(8,128)(2,1)S(1)}, bf16[4,1024,512]{2,1,0:T(8,128)(2,1)}, u32[]{:S(2)}) %copy-start) | copy-done | bytes 4194328
  27.4 2.2 %copy-done.1 = bf16[4,1024,512]{2,1,0:T(8,128)(2,1)S(1)} copy-done((bf16[4,1024,512]{2,1,0:T(8,128)(2,1)S(1)}, bf16[4,1024,512]{2,1,0:T(8,128)(2,1)}, u32[]{:S(2)}) %copy-start.1) | copy-done | bytes 4194328
  29.5 8.9 %shard_map.91 = bf16[512,1024]{1,0:T(8,128)(2,1)S(1)} custom-call(bf16[512,1024]{1,0:T(8,128)(2,1)S(1)} %slice.36.rows_ref, f32[512,128]{1,0:T(8,128)S(1)} %pad_convert_fusion.weight_ref, bf16[4,1024,512]{2,1,0:T(8,128)(2,1)S(1)} %copy-done, bf16[4,1024,512]{2,1,0:T(8,128)(2,1)S(1)} %copy-done.1, bf16[4,512,1024]{2,1,0:T(8,128)(2,1)} %down_ref.1), custom_call_target="tpu_custom_call" | custom-call | tf_op jit(solution)/shard_map/pallas_call | solution.py:38
  38.7 1.8 %collective-permute-done.5 = bf16[256,1024]{1,0:T(8,128)(2,1)S(1)} collective-permute-done((bf16[256,1024]{1,0:T(8,128)(2,1)S(1)}, bf16[256,1024]{1,0:T(8,128)(2,1)S(1)}, u32[]{:S(2)}, u32[]{:S(2)}) %collective-permute-start.5) | collective-permute-done | bytes 524320 | tf_op jit(solution)/shard_map/ppermute | solution.py:98
  40.7 1.6 %collective-permute-start.6 = (bf16[256,512]{1,0:T(8,128)(2,1)S(1)}, bf16[256,512]{1,0:T(8,128)(2,1)S(1)}, u32[]{:S(2)}, u32[]{:S(2)}) collective-permute-start(bf16[256,512]{1,0:T(8,128)(2,1)S(1)} %constant_dynamic-slice_fusion), channel_id=1, source_target_pairs={{0,1},{1,0},{2,3},{3,2},{4,5},{5,4},{6,7},{7,6},{8,9},{9,8},{10,11... | collective-permute-start | bytes 786440 | tf_op jit(solution)/shard_map/ppermute | solution.py:56
  42.3 6.9 %collective-permute-done.6 = bf16[256,512]{1,0:T(8,128)(2,1)S(1)} collective-permute-done((bf16[256,512]{1,0:T(8,128)(2,1)S(1)}, bf16[256,512]{1,0:T(8,128)(2,1)S(1)}, u32[]{:S(2)}, u32[]{:S(2)}) %collective-permute-start.6) | collective-permute-done | bytes 262176 | tf_op jit(solution)/shard_map/ppermute | solution.py:56
  49.3 4.7 %collective-permute-start.7 = (bf16[64,512]{1,0:T(8,128)(2,1)S(1)}, bf16[64,512]{1,0:T(8,128)(2,1)S(1)}, u32[]{:S(2)}, u32[]{:S(2)}) collective-permute-start(bf16[64,512]{1,0:T(8,128)(2,1)S(1)} %get-tuple-element.5), channel_id=1, source_target_pairs={{0,12},{2,14},{4,0},{6,2},{8,4},{10,6},{12,8},{14,10},{1,13},{3,15... | collective-permute-start | bytes 196616 | tf_op jit(solution)/shard_map/ppermute | solution.py:56
  54.0 0.4 collective-permute-start.8
  54.7 1.5 %collective-permute-done.7 = bf16[64,512]{1,0:T(8,128)(2,1)S(1)} collective-permute-done((bf16[64,512]{1,0:T(8,128)(2,1)S(1)}, bf16[64,512]{1,0:T(8,128)(2,1)S(1)}, u32[]{:S(2)}, u32[]{:S(2)}) %collective-permute-start.7) | collective-permute-done | bytes 65568 | tf_op jit(solution)/shard_map/ppermute | solution.py:56
  56.2 3.4 %collective-permute-done.8 = bf16[64,512]{1,0:T(8,128)(2,1)S(1)} collective-permute-done((bf16[64,512]{1,0:T(8,128)(2,1)S(1)}, bf16[64,512]{1,0:T(8,128)(2,1)S(1)}, u32[]{:S(2)}, u32[]{:S(2)}) %collective-permute-start.8) | collective-permute-done | bytes 65568 | tf_op jit(solution)/shard_map/ppermute | solution.py:56
  59.7 0.8 %collective-permute-done.9 = bf16[64,512]{1,0:T(8,128)(2,1)S(1)} collective-permute-done((bf16[64,512]{1,0:T(8,128)(2,1)S(1)}, bf16[64,512]{1,0:T(8,128)(2,1)S(1)}, u32[]{:S(2)}, u32[]{:S(2)}) %collective-permute-start.9) | collective-permute-done | bytes 65568 | tf_op jit(solution)/shard_map/ppermute | solution.py:56
  60.6 2.1 %convolution_convert_fusion = bf16[64,2048]{1,0:T(8,128)(2,1)S(1)} fusion(bf16[64,512]{1,0:T(8,128)(2,1)S(1)} %divide_convert_fusion, bf16[512,4096]{1,0:T(8,128)(2,1)} %param.17, s32[]{:T(128)S(6)} %select_n.33), kind=kOutput, calls=%fused_computation | convolution fusion | flops 134348800 | bytes 2424836 | tf_op jit(solution)/shard_map/dot_general | solution.py:145
  62.7 1.5 %collective-permute-start.10 = (bf16[64,2048]{1,0:T(8,128)(2,1)S(1)}, bf16[64,2048]{1,0:T(8,128)(2,1)S(1)}, u32[]{:S(2)}, u32[]{:S(2)}) collective-permute-start(bf16[64,2048]{1,0:T(8,128)(2,1)S(1)} %convolution_convert_fusion), channel_id=1, source_target_pairs={{0,1},{1,0},{2,3},{3,2},{4,5},{5,4},{6,7},{7,6},{8,9},{9,8},{10,11... | collective-permute-start | bytes 786440 | tf_op jit(solution)/shard_map/ppermute | solution.py:56
  64.2 5.6 %collective-permute-done.10 = bf16[64,2048]{1,0:T(8,128)(2,1)S(1)} collective-permute-done((bf16[64,2048]{1,0:T(8,128)(2,1)S(1)}, bf16[64,2048]{1,0:T(8,128)(2,1)S(1)}, u32[]{:S(2)}, u32[]{:S(2)}) %collective-permute-start.10) | collective-permute-done | bytes 262176 | tf_op jit(solution)/shard_map/ppermute | solution.py:56
  69.9 2.8 %add_convert_fusion.1 = bf16[64,2048]{1,0:T(8,128)(2,1)} fusion(bf16[64,2048]{1,0:T(8,128)(2,1)S(1)} %collective-permute-done.10, bf16[64,2048]{1,0:T(8,128)(2,1)S(1)} %bitcast.11, bf16[64,512]{1,0:T(8,128)(2,1)S(1)} %divide_convert_fusion, bf16[512,4096]{1,0:T(8,128)(2,1)} %param.17, s32[]{:T(128)S(6)} %select_n.34), kind=kOutput, calls=%fused_computation.8 | convolution fusion | flops 134873088 | bytes 2949124 | tf_op jit(solution)/shard_map/dot_general | solution.py:151
  (42 shorter events, 2.2 us)
Async XLA Ops:
  0.0 6.2 %copy-start.3 = (s32[2,32,16]{1,2,0:T(8,128)S(1)}, s32[2,32,16]{1,2,0:T(8,128)}, u32[]{:S(2)}) copy-start(s32[2,32,16]{1,2,0:T(8,128)} %param.11) | copy-start | bytes 12292
  0.0 6.3 %copy-start.4 = (s32[2,32,16]{1,2,0:T(8,128)S(1)}, s32[2,32,16]{1,2,0:T(8,128)}, u32[]{:S(2)}) copy-start(s32[2,32,16]{1,2,0:T(8,128)} %param.10) | copy-start | bytes 12292
  0.0 6.4 %copy-start.5 = (s32[32]{0:T(128)S(1)}, s32[32]{0:T(128)}, u32[]{:S(2)}) copy-start(s32[32]{0:T(128)} %param.12) | copy-start | bytes 388
  3.2 6.5 %collective-permute-start = (bf16[64,1024]{1,0:T(8,128)(2,1)S(1)}, bf16[64,1024]{1,0:T(8,128)(2,1)S(1)}, u32[]{:S(2)}, u32[]{:S(2)}) collective-permute-start(bf16[64,1024]{1,0:T(8,128)(2,1)S(1)} %convolution_convert_fusion.1), channel_id=1, source_target_pairs={{0,1},{1,0},{2,3},{3,2},{4,5},{5,4},{6,7},{7,6},{8,9},{9,8},{10,11... | collective-permute-start | bytes 393224 | tf_op jit(solution)/shard_map/ppermute | solution.py:56
  9.7 8.8 %collective-permute-start.1 = (bf16[64,1152]{1,0:T(8,128)(2,1)S(1)}, bf16[64,1152]{1,0:T(8,128)(2,1)S(1)}, u32[]{:S(2)}, u32[]{:S(2)}) collective-permute-start(bf16[64,1152]{1,0:T(8,128)(2,1)S(1)} %get-tuple-element.8), channel_id=1, source_target_pairs={{0,4},{2,6},{4,8},{6,10},{8,12},{10,14},{12,0},{14,2},{1,5},{3,7},... | collective-permute-start | bytes 442376 | tf_op jit(solution)/shard_map/ppermute | solution.py:56
  11.6 11.4 %collective-permute-start.2 = (bf16[64,1152]{1,0:T(8,128)(2,1)S(1)}, bf16[64,1152]{1,0:T(8,128)(2,1)S(1)}, u32[]{:S(2)}, u32[]{:S(2)}) collective-permute-start(bf16[64,1152]{1,0:T(8,128)(2,1)S(1)} %get-tuple-element.8), channel_id=1, source_target_pairs={{0,8},{2,10},{4,12},{6,14},{8,0},{10,2},{12,4},{14,6},{1,9},{3,11}... | collective-permute-start | bytes 442376 | tf_op jit(solution)/shard_map/ppermute | solution.py:56
  14.2 8.8 %collective-permute-start.3 = (bf16[64,1152]{1,0:T(8,128)(2,1)S(1)}, bf16[64,1152]{1,0:T(8,128)(2,1)S(1)}, u32[]{:S(2)}, u32[]{:S(2)}) collective-permute-start(bf16[64,1152]{1,0:T(8,128)(2,1)S(1)} %get-tuple-element.8), channel_id=1, source_target_pairs={{0,12},{2,14},{4,0},{6,2},{8,4},{10,6},{12,8},{14,10},{1,13},{3,15... | collective-permute-start | bytes 442376 | tf_op jit(solution)/shard_map/ppermute | solution.py:56
  23.1 2.1 %collective-permute-start.4 = (bf16[256,1152]{1,0:T(8,128)(2,1)S(1)}, bf16[256,1152]{1,0:T(8,128)(2,1)S(1)}, u32[]{:S(2)}, u32[]{:S(2)}) collective-permute-start(bf16[256,1152]{1,0:T(8,128)(2,1)S(1)} %pad_maximum_fusion), channel_id=1, source_target_pairs={{0,2},{2,0},{4,6},{6,4},{8,10},{10,8},{12,14},{14,12},{1,3},{3,1},... | collective-permute-start | bytes 1769480 | tf_op jit(solution)/shard_map/ppermute | solution.py:98
  25.2 2.2 %copy-start = (bf16[4,1024,512]{2,1,0:T(8,128)(2,1)S(1)}, bf16[4,1024,512]{2,1,0:T(8,128)(2,1)}, u32[]{:S(2)}) copy-start(bf16[4,1024,512]{2,1,0:T(8,128)(2,1)} %gate_ref.1) | copy-start | bytes 12582916
  27.4 2.2 %copy-start.1 = (bf16[4,1024,512]{2,1,0:T(8,128)(2,1)S(1)}, bf16[4,1024,512]{2,1,0:T(8,128)(2,1)}, u32[]{:S(2)}) copy-start(bf16[4,1024,512]{2,1,0:T(8,128)(2,1)} %up_ref.1) | copy-start | bytes 12582916
  38.5 2.0 %collective-permute-start.5 = (bf16[256,1024]{1,0:T(8,128)(2,1)S(1)}, bf16[256,1024]{1,0:T(8,128)(2,1)S(1)}, u32[]{:S(2)}, u32[]{:S(2)}) collective-permute-start(bf16[256,1024]{1,0:T(8,128)(2,1)S(1)} %slice.39), channel_id=1, source_target_pairs={{0,2},{2,0},{4,6},{6,4},{8,10},{10,8},{12,14},{14,12},{1,3},{3,1},... | collective-permute-start | bytes 1572872 | tf_op jit(solution)/shard_map/ppermute | solution.py:98
  40.7 8.4 %collective-permute-start.6 = (bf16[256,512]{1,0:T(8,128)(2,1)S(1)}, bf16[256,512]{1,0:T(8,128)(2,1)S(1)}, u32[]{:S(2)}, u32[]{:S(2)}) collective-permute-start(bf16[256,512]{1,0:T(8,128)(2,1)S(1)} %constant_dynamic-slice_fusion), channel_id=1, source_target_pairs={{0,1},{1,0},{2,3},{3,2},{4,5},{5,4},{6,7},{7,6},{8,9},{9,8},{10,11... | collective-permute-start | bytes 786440 | tf_op jit(solution)/shard_map/ppermute | solution.py:56
  49.3 7.0 %collective-permute-start.7 = (bf16[64,512]{1,0:T(8,128)(2,1)S(1)}, bf16[64,512]{1,0:T(8,128)(2,1)S(1)}, u32[]{:S(2)}, u32[]{:S(2)}) collective-permute-start(bf16[64,512]{1,0:T(8,128)(2,1)S(1)} %get-tuple-element.5), channel_id=1, source_target_pairs={{0,12},{2,14},{4,0},{6,2},{8,4},{10,6},{12,8},{14,10},{1,13},{3,15... | collective-permute-start | bytes 196616 | tf_op jit(solution)/shard_map/ppermute | solution.py:56
  54.0 5.7 %collective-permute-start.8 = (bf16[64,512]{1,0:T(8,128)(2,1)S(1)}, bf16[64,512]{1,0:T(8,128)(2,1)S(1)}, u32[]{:S(2)}, u32[]{:S(2)}) collective-permute-start(bf16[64,512]{1,0:T(8,128)(2,1)S(1)} %get-tuple-element.7), channel_id=1, source_target_pairs={{0,8},{2,10},{4,12},{6,14},{8,0},{10,2},{12,4},{14,6},{1,9},{3,11}... | collective-permute-start | bytes 196616 | tf_op jit(solution)/shard_map/ppermute | solution.py:56
  54.4 6.1 %collective-permute-start.9 = (bf16[64,512]{1,0:T(8,128)(2,1)S(1)}, bf16[64,512]{1,0:T(8,128)(2,1)S(1)}, u32[]{:S(2)}, u32[]{:S(2)}) collective-permute-start(bf16[64,512]{1,0:T(8,128)(2,1)S(1)} %get-tuple-element.6), channel_id=1, source_target_pairs={{0,4},{2,6},{4,8},{6,10},{8,12},{10,14},{12,0},{14,2},{1,5},{3,7},... | collective-permute-start | bytes 196616 | tf_op jit(solution)/shard_map/ppermute | solution.py:56
  60.5 9.3 %copy-start.2 = (bf16[2,32,2048]{2,1,0:T(8,128)(2,1)S(1)}, bf16[2,32,2048]{2,1,0:T(8,128)(2,1)}, u32[]{:S(2)}) copy-start(bf16[2,32,2048]{2,1,0:T(8,128)(2,1)} %param.9) | copy-start | bytes 786436
  62.7 7.2 %collective-permute-start.10 = (bf16[64,2048]{1,0:T(8,128)(2,1)S(1)}, bf16[64,2048]{1,0:T(8,128)(2,1)S(1)}, u32[]{:S(2)}, u32[]{:S(2)}) collective-permute-start(bf16[64,2048]{1,0:T(8,128)(2,1)S(1)} %convolution_convert_fusion), channel_id=1, source_target_pairs={{0,1},{1,0},{2,3},{3,2},{4,5},{5,4},{6,7},{7,6},{8,9},{9,8},{10,11... | collective-permute-start | bytes 786440 | tf_op jit(solution)/shard_map/ppermute | solution.py:56

commit v2 on v1

v2 whole, which is shorter than its diff:
```python
import functools

import jax
import jax.numpy as jnp
from jax import lax
from jax.experimental import pallas as pl
from jax.experimental.pallas import tpu as pltpu
from jax.sharding import PartitionSpec as P

LANES = 128
VMEM_LIMIT = 24 * 1024 * 1024
CHEAP = pl.CostEstimate(flops=1, bytes_accessed=1, transcendentals=0)


def whole(count):
    return [pl.BlockSpec(memory_space=pltpu.VMEM)] * count


def call(kernel, out_shape, *operands):
    shapes = [jax.ShapeDtypeStruct(shape, dtype) for shape, dtype in out_shape]
    return pl.pallas_call(
        kernel,
        in_specs=whole(len(operands)),
        out_specs=whole(len(shapes)),
        out_shape=shapes,
        compiler_params=pltpu.CompilerParams(vmem_limit_bytes=VMEM_LIMIT),
        cost_estimate=CHEAP,
    )(*operands)


def fetch_kernel(mark_ref, *refs):
    count = len(refs) // 2
    sems = refs[-1]
    copies = [pltpu.make_async_copy(refs[i], refs[count + i], sems.at[i]) for i in range(count)]
    for copy in copies:
        copy.start()
    for copy in copies:
        copy.wait()


def fetch(mark, *arrays):
    held = [pltpu.with_memory_space_constraint(a, pltpu.HBM) for a in arrays]
    return pl.pallas_call(
        fetch_kernel,
        in_specs=[pl.BlockSpec(memory_space=pl.ANY)]
        + [pl.BlockSpec(memory_space=pltpu.HBM)] * len(arrays),
        out_specs=whole(len(arrays)),
        out_shape=[pltpu.VMEM(a.shape, a.dtype) for a in arrays],
        scratch_shapes=[pltpu.SemaphoreType.DMA((len(arrays),))],
        compiler_params=pltpu.CompilerParams(vmem_limit_bytes=1024 * 1024),
        cost_estimate=CHEAP,
    )(mark, *held)


def route_kernel(ids_ref, route_ref, slot_ref, weight_ref, norm_ref):
    steps, top_count, rows = ids_ref.shape
    slots, padded = slot_ref.shape[1], weight_ref.shape[1]
    every = lax.broadcasted_iota(jnp.int32, (slots, rows), 0)
    move = lax.broadcasted_iota(jnp.int32, (padded, slots), 0) == slot_ref[...]
    move = jnp.where(move, 1.0, 0.0).astype(jnp.bfloat16)
    for s in range(steps):
        ids, route = ids_ref[s], route_ref[s].astype(jnp.float32)
        by_expert = jnp.zeros((slots, rows), jnp.float32)
        for k in range(top_count):
            by_expert = by_expert + jnp.where(every == ids[k : k + 1], route[k : k + 1], 0.0)
        by_slot = jnp.dot(move, by_expert.astype(jnp.bfloat16), preferred_element_type=jnp.float32)
        at = pl.ds(s * rows, rows)
        weight_ref[at, :] = by_slot.T.astype(jnp.bfloat16)
        norm = jnp.broadcast_to(jnp.sum(route, axis=0, keepdims=True), (norm_ref.shape[1], rows))
        norm_ref[at, :] = norm.T


def expert_kernel(own_ref, pair_ref, gate_ref, up_ref, down_ref, own_out_ref, pair_out_ref):
    local_count, width = gate_ref.shape[0], gate_ref.shape[1]
    both = jnp.concatenate([own_ref[...], pair_ref[...]], axis=0)
    rows, weights = both[:, :width], both[:, width:].astype(jnp.float32)
    lanes = lax.broadcasted_iota(jnp.int32, weights.shape, 1)
    first = lax.axis_index("expert") * local_count
    total = None
    for j in range(local_count):
        gate_act = jnp.dot(rows, gate_ref[j], preferred_element_type=jnp.float32)
        up_act = jnp.dot(rows, up_ref[j], preferred_element_type=jnp.float32)
        weight = jnp.sum(jnp.where(lanes == first + j, weights, 0.0), axis=1, keepdims=True)
        hidden = (gate_act / (1.0 + jnp.exp(-gate_act)) * up_act * weight).astype(jnp.bfloat16)
        term = jnp.dot(hidden, down_ref[j], preferred_element_type=jnp.float32)
        total = term if total is None else total + term
    total = total.astype(jnp.bfloat16)
    half = own_out_ref.shape[0]
    own_out_ref[...] = total[:half]
    pair_out_ref[...] = total[half:]


def fold_kernel(tensor_count, *refs):
    terms, outs = refs[:-tensor_count], refs[-tensor_count:]
    me = lax.axis_index("tensor")
    width = outs[0].shape[1]
    for s, out in enumerate(outs):
        at = pl.multiple_of(lax.rem(me + s, tensor_count) * width, width)
        total = terms[0][:, pl.ds(at, width)].astype(jnp.float32)
        for term in terms[1:]:
            total = total + term[:, pl.ds(at, width)].astype(jnp.float32)
        out[...] = total.astype(out.dtype)


def away_kernel(tensor_count, norm_ref, up_ref, *refs):
    pieces, mixed_ref, outs = refs[:-tensor_count], refs[-tensor_count], refs[1 - tensor_count :]
    total = pieces[0][...].astype(jnp.float32)
    for piece in pieces[1:]:
        total = total + piece[...].astype(jnp.float32)
    mixed = (total / norm_ref[:, :1]).astype(jnp.bfloat16)
    mixed_ref[...] = mixed
    me = lax.axis_index("tensor")
    for s, out in enumerate(outs):
        width = out.shape[1]
        at = pl.multiple_of(lax.rem(me + s + 1, tensor_count) * width, width)
        out[...] = jnp.dot(
            mixed, up_ref[:, pl.ds(at, width)], preferred_element_type=jnp.float32
        ).astype(out.dtype)


def held_kernel(up_ref, mixed_ref, inputs_ref, held_ref):
    width = held_ref.shape[1]
    at = pl.multiple_of(lax.axis_index("tensor") * width, width)
    held_ref[...] = inputs_ref[...].astype(jnp.float32) + jnp.dot(
        mixed_ref[...], up_ref[:, pl.ds(at, width)], preferred_element_type=jnp.float32
    )


def add(*terms):
    return functools.reduce(jnp.add, [t.astype(jnp.float32) for t in terms])


def shards(
    tokens,
    expert_ids,
    route_weights,
    expert_slot,
    latent_down,
    gate_proj,
    up_proj,
    down_proj,
    latent_up,
):
    steps, step_rows, features = tokens.shape
    rows = steps * step_rows
    latent_width = latent_down.shape[1]
    tensor_count = lax.axis_size("tensor")
    expert_axis = lax.axis_size("expert")
    pair = 2 if expert_axis % 2 == 0 else 1
    far = expert_axis // pair
    block = latent_width // tensor_count

    def across(x, s):
        return lax.ppermute(
            x, "tensor", [(i, (i + s) % tensor_count) for i in range(tensor_count)]
        )

    def swap(x):
        return lax.ppermute(x, "expert", [(i, i ^ 1) for i in range(expert_axis)])

    def far_swap(x, s, back=False):
        if far & (far - 1) == 0:
            return lax.ppermute(x, "expert", [(i, i ^ (s * pair)) for i in range(expert_axis)])
        by = (-s if back else s) * pair
        return lax.ppermute(x, "expert", [(i, (i + by) % expert_axis) for i in range(expert_axis)])

    inputs = tokens.reshape(rows, features)
    slots = expert_slot.shape[0]
    weights, norm = call(
        route_kernel,
        [((rows, -(-slots // LANES) * LANES), jnp.bfloat16), ((rows, LANES), jnp.float32)],
        expert_ids.transpose(0, 2, 1),
        route_weights.transpose(0, 2, 1),
        expert_slot.reshape(1, slots),
    )
    partial = jnp.dot(inputs, latent_down, preferred_element_type=jnp.float32).astype(jnp.bfloat16)
    latent = add(partial, *[across(partial, s) for s in range(1, tensor_count)])
    (gate_proj,) = fetch(partial, gate_proj)
    latent, weights, gate_proj = lax.optimization_barrier((latent, weights, gate_proj))
    payload = jnp.concatenate([latent.astype(jnp.bfloat16), weights], axis=1)
    blocks = [payload] + [far_swap(payload, s) for s in range(1, far)]
    up_proj, down_proj = fetch(payload, up_proj, down_proj)
    *blocks, up_proj, down_proj = lax.optimization_barrier((*blocks, up_proj, down_proj))

    def apply(own, other):
        shape = ((own.shape[0], latent_width), jnp.bfloat16)
        return call(expert_kernel, [shape] * 2, own, other, gate_proj, up_proj, down_proj)

    def fold(*terms):
        shape = ((terms[0].shape[0], block), jnp.bfloat16)
        return call(functools.partial(fold_kernel, tensor_count), [shape] * tensor_count, *terms)

    def halves(own):
        return (own, swap(own)) if pair == 2 else jnp.split(own, 2, axis=0)

    def join(own, other):
        return fold(own, swap(other)) if pair == 2 else fold(jnp.concatenate([own, other], axis=0))

    cut = far // 2
    pieces = []
    for part in (blocks[cut:], blocks[:cut]) if cut else (blocks,):
        own = jnp.concatenate(part, axis=0)
        held, *away = join(*apply(*halves(own)))
        arrived = [across(x, s + 1) for s, x in enumerate(away)]
        sums = add(held, *arrived).astype(jnp.bfloat16)
        pieces = [sums[i : i + rows] for i in range(0, sums.shape[0], rows)] + pieces
    (latent_up,) = fetch(pieces[-1], latent_up)
    pieces = [pieces[0]] + [far_swap(pieces[s], s, back=True) for s in range(1, far)]

    mixed_rows, *away = call(
        functools.partial(away_kernel, tensor_count),
        [((rows, block), jnp.bfloat16)] + [((rows, features), jnp.bfloat16)] * (tensor_count - 1),
        norm,
        latent_up,
        *pieces,
    )
    arrived = [across(x, s + 1) for s, x in enumerate(away)]
    (held,) = call(
        held_kernel, [((rows, features), jnp.float32)], latent_up, mixed_rows, inputs
    )
    return add(held, *arrived).astype(jnp.bfloat16).reshape(steps, step_rows, features)


def solution(mesh):
    in_specs = (
        P(None, ("groups", "expert", "dp"), "tensor"),
        P(None, ("groups", "expert", "dp"), None),
        P(None, ("groups", "expert", "dp"), None),
        P(),
        P("tensor", None),
        P("expert", None, "tensor"),
        P("expert", None, "tensor"),
        P("expert", "tensor", None),
        P("tensor", None),
    )
    out_specs = P(None, ("groups", "expert", "dp"), "tensor")
    return jax.shard_map(shards, mesh=mesh, in_specs=in_specs, out_specs=out_specs, check_vma=False)
```

time: 73 us -> 59.2 us (0.81)
  waiting for transfers between devices: 32.3 us -> 22.4 us
  Pallas kernels: 8.93 us -> 16.7 us
  matrix products: 8.31 us -> 3.12 us
  local copies, waits for them, and re-layouts: 4.85 us -> 0.11 us
  starting transfers between devices: 17.6 us -> 15.7 us
    pallas_call x1 -> x10, Pallas kernels: 8.93 us -> 16.7 us  [the longest x7 8.79 us: call(): pl.pallas_call(kernel, in_specs=whole(len(operands)), out_specs=whole(len...]
    ppermute x9 -> x10, waiting for transfers between devices: 28.6 us -> 21.4 us  [the longest x4 11.3 us: across(): lax.ppermute(x, 'tensor', [(i, (i + s) % tensor_count) for i in range(ten...]
    dot_general x3 -> x0, matrix products: 5.15 us -> none  [the longest x1 2.78 us: shards(): jnp.dot(mixed_rows, features_of(latent_up, tensor_index, features), prefe...]
    unnamed x17 -> x10, local copies, waits for them, and re-layouts: 4.09 us -> 0.05 us
    ppermute x9 -> x10, starting transfers between devices: 17.3 us -> 14.4 us  [the longest x6 7.25 us: far_swap(): lax.ppermute(x, 'expert', [(i, i ^ s * pair) for i in range(expert_axis)])]
    ppermute x2 -> x4, waiting for transfers between devices: 3.69 us -> 1 us  [swap(): return lax.ppermute(x, 'expert', [(i, i ^ 1) for i in range(expert_axis)])]
    ppermute x2 -> x4, starting transfers between devices: 0.28 us -> 1.27 us  [swap(): return lax.ppermute(x, 'expert', [(i, i ^ 1) for i in range(expert_axis)])]
  transfers between devices with their start and end apart: 11 -> 14, of which waited for: 10 -> 8; matrix products, arithmetic and copies ran while one was open for 1% -> 0% of each run, Pallas kernels for 0% -> 27%
where the time goes in v2:
time: 59.2 us; the launch traced here: 59 us
  waiting for transfers between devices  22.4 us (38%)
  Pallas kernels  16.7 us (28%)
  starting transfers between devices  15.7 us (27%)
  matrix products  3.12 us (5%)
  other arithmetic  0.87 us (1%)
    ppermute x4, waiting for transfers between devices, across(): lax.ppermute(x, 'tensor', [(i, (i + s) % tensor_count) for i in range(ten...  11.3 us
    ppermute x6, waiting for transfers between devices, far_swap(): lax.ppermute(x, 'expert', [(i, i ^ s * pair) for i in range(expert_axis)])  10.1 us
    pallas_call x7, Pallas kernels, call(): pl.pallas_call(kernel, in_specs=whole(len(operands)), out_specs=whole(len...  8.79 us
    pallas_call x3, Pallas kernels, fetch(): pl.pallas_call(fetch_kernel, in_specs=[pl.BlockSpec(memory_space=pl.ANY)]...  7.87 us
    ppermute x6, starting transfers between devices, far_swap(): lax.ppermute(x, 'expert', [(i, i ^ s * pair) for i in range(expert_axis)])  7.25 us
    ppermute x4, starting transfers between devices, across(): lax.ppermute(x, 'tensor', [(i, (i + s) % tensor_count) for i in range(ten...  7.2 us
    dot_general x1, matrix products, shards(): jnp.dot(inputs, latent_down, preferred_element_type=jnp.float32)  3.12 us
    ppermute x4, starting transfers between devices, swap(): return lax.ppermute(x, 'expert', [(i, i ^ 1) for i in range(expert_axis)])  1.27 us
  transfers between devices with their start and end apart: 14, of which 8 were waited for; matrix products, arithmetic and copies ran while one was open for 0% of the time, Pallas kernels for 27%

profile of v2, /device:TPU:0, one launch (start us, length us, event | category | flops | bytes accessed | tf_op | source)
XLA Modules:
  0.0 59.0 jit_solution(1177056676850205441)
XLA Ops:
  0.0 3.1 %convolution_convert_fusion.mark_ref = bf16[64,1024]{1,0:T(8,128)(2,1)S(1)} fusion(bf16[64,2048]{1,0:T(8,128)(2,1)} %bitcast.7, bf16[2048,1024]{1,0:T(8,128)(2,1)} %param.13), kind=kOutput, calls=%fused_computation | convolution fusion | flops 268500992 | bytes 4587520 | tf_op jit(solution)/shard_map/dot_general | solution.py:176
  3.2 3.0 %collective-permute-start = (bf16[64,1024]{1,0:T(8,128)(2,1)S(1)}, bf16[64,1024]{1,0:T(8,128)(2,1)S(1)}, u32[]{:S(2)}, u32[]{:S(2)}) collective-permute-start(bf16[64,1024]{1,0:T(8,128)(2,1)S(1)} %convolution_convert_fusion.mark_ref), channel_id=1, source_target_pairs={{0,1},{1,0},{2,3},{3,2},{4,5},{5,4},{6,7},{7,6},{8,9},{9,8},{10,11... | collective-permute-start | bytes 393224 | tf_op jit(solution)/shard_map/ppermute | solution.py:154
  6.2 2.2 %shard_map.92.gate_ref = bf16[4,1024,512]{2,1,0:T(8,128)(2,1)S(1)} custom-call(bf16[64,1024]{1,0:T(8,128)(2,1)S(1)} %convolution_convert_fusion.mark_ref, bf16[4,1024,512]{2,1,0:T(8,128)(2,1)} %refs_0_.3), custom_call_target="tpu_custom_call" | custom-call | flops 1 | bytes 1 | tf_op jit(solution)/shard_map/pallas_call | solution.py:43
  8.7 1.0 %collective-permute-done = bf16[64,1024]{1,0:T(8,128)(2,1)S(1)} collective-permute-done((bf16[64,1024]{1,0:T(8,128)(2,1)S(1)}, bf16[64,1024]{1,0:T(8,128)(2,1)S(1)}, u32[]{:S(2)}, u32[]{:S(2)}) %collective-permute-start) | collective-permute-done | bytes 131104 | tf_op jit(solution)/shard_map/ppermute | solution.py:154
  9.7 3.9 %collective-permute-start.3 = (bf16[64,1152]{1,0:T(8,128)(2,1)S(1)}, bf16[64,1152]{1,0:T(8,128)(2,1)S(1)}, u32[]{:S(2)}, u32[]{:S(2)}) collective-permute-start(bf16[64,1152]{1,0:T(8,128)(2,1)S(1)} %pad_maximum_fusion.mark_ref), channel_id=1, source_target_pairs={{0,12},{2,14},{4,8},{6,10},{8,4},{10,6},{12,0},{14,2},{1,13},{3,15... | collective-permute-start | bytes 442376 | tf_op jit(solution)/shard_map/ppermute | solution.py:163
  13.6 0.6 %collective-permute-start.1 = (bf16[64,1152]{1,0:T(8,128)(2,1)S(1)}, bf16[64,1152]{1,0:T(8,128)(2,1)S(1)}, u32[]{:S(2)}, u32[]{:S(2)}) collective-permute-start(bf16[64,1152]{1,0:T(8,128)(2,1)S(1)} %pad_maximum_fusion.mark_ref), channel_id=1, source_target_pairs={{0,4},{2,6},{4,0},{6,2},{8,12},{10,14},{12,8},{14,10},{1,5},{3,7},... | collective-permute-start | bytes 442376 | tf_op jit(solution)/shard_map/ppermute | solution.py:163
  14.3 3.5 %shard_map.93 = (bf16[4,1024,512]{2,1,0:T(8,128)(2,1)S(1)}, bf16[4,512,1024]{2,1,0:T(8,128)(2,1)S(1)}) custom-call(bf16[64,1152]{1,0:T(8,128)(2,1)S(1)} %pad_maximum_fusion.mark_ref, bf16[4,1024,512]{2,1,0:T(8,128)(2,1)} %refs_0_.4, bf16[4,512,1024]{2,1,0:T(8,128)(2,1)} %refs_1_.1), custom_call_target="tpu_custom_call" | custom-call | flops 1 | bytes 1 | tf_op jit(solution)/shard_map/pallas_call | solution.py:43
  17.8 0.6 %collective-permute-done.3 = bf16[64,1152]{1,0:T(8,128)(2,1)S(1)} collective-permute-done((bf16[64,1152]{1,0:T(8,128)(2,1)S(1)}, bf16[64,1152]{1,0:T(8,128)(2,1)S(1)}, u32[]{:S(2)}, u32[]{:S(2)}) %collective-permute-start.3) | collective-permute-done | bytes 147488 | tf_op jit(solution)/shard_map/ppermute | solution.py:163
  18.4 6.8 %collective-permute-done.2 = bf16[64,1152]{1,0:T(8,128)(2,1)S(1)} collective-permute-done((bf16[64,1152]{1,0:T(8,128)(2,1)S(1)}, bf16[64,1152]{1,0:T(8,128)(2,1)S(1)}, u32[]{:S(2)}, u32[]{:S(2)}) %collective-permute-start.2) | collective-permute-done | bytes 147488 | tf_op jit(solution)/shard_map/ppermute | solution.py:163
  25.4 0.6 collective-permute-start.4
  26.0 1.0 %collective-permute-done.7.pair_ref = bf16[128,1152]{1,0:T(8,128)(2,1)S(1)} collective-permute-done((bf16[128,1152]{1,0:T(8,128)(2,1)S(1)}, bf16[128,1152]{1,0:T(8,128)(2,1)S(1)}, u32[]{:S(2)}, u32[]{:S(2)}) %collective-permute-start.7) | collective-permute-done | bytes 294944 | tf_op jit(solution)/shard_map/ppermute | solution.py:159
  27.0 3.7 %shard_map.97 = (bf16[128,1024]{1,0:T(8,128)(2,1)S(1)}, bf16[128,1024]{1,0:T(8,128)(2,1)S(1)}) custom-call(bf16[128,1152]{1,0:T(8,128)(2,1)S(1)} %constant_dynamic-update-slice_fusion.2.own_ref, bf16[128,1152]{1,0:T(8,128)(2,1)S(1)} %collective-permute-done.7.pair_ref, bf16[4,1024,512]{2,1,0:T(8,128)(2,1)S(1)} %shard_map.92.gate_ref, ...), custom_call_target="tpu_custom_call" | custom-call | flops 1 | bytes 1 | tf_op jit(solution)/shard_map/pallas_call | solution.py:21
  30.9 3.7 %shard_map.94 = (bf16[128,1024]{1,0:T(8,128)(2,1)S(1)}, bf16[128,1024]{1,0:T(8,128)(2,1)S(1)}) custom-call(bf16[128,1152]{1,0:T(8,128)(2,1)S(1)} %constant_dynamic-update-slice_fusion.own_ref, bf16[128,1152]{1,0:T(8,128)(2,1)S(1)} %collective-permute-done.4.pair_ref, bf16[4,1024,512]{2,1,0:T(8,128)(2,1)S(1)} %shard_map.92.gate_ref, ...), custom_call_target="tpu_custom_call" | custom-call | flops 1 | bytes 1 | tf_op jit(solution)/shard_map/pallas_call | solution.py:21
  35.1 1.6 %collective-permute-start.9 = (bf16[128,512]{1,0:T(8,128)(2,1)S(1)}, bf16[128,512]{1,0:T(8,128)(2,1)S(1)}, u32[]{:S(2)}, u32[]{:S(2)}) collective-permute-start(bf16[128,512]{1,0:T(8,128)(2,1)S(1)} %get-tuple-element.48), channel_id=1, source_target_pairs={{0,1},{1,0},{2,3},{3,2},{4,5},{5,4},{6,7},{7,6},{8,9},{9,8},{10,11... | collective-permute-start | bytes 393224 | tf_op jit(solution)/shard_map/ppermute | solution.py:154
  36.7 1.1 %collective-permute-start.6 = (bf16[128,512]{1,0:T(8,128)(2,1)S(1)}, bf16[128,512]{1,0:T(8,128)(2,1)S(1)}, u32[]{:S(2)}, u32[]{:S(2)}) collective-permute-start(bf16[128,512]{1,0:T(8,128)(2,1)S(1)} %get-tuple-element.41), channel_id=1, source_target_pairs={{0,1},{1,0},{2,3},{3,2},{4,5},{5,4},{6,7},{7,6},{8,9},{9,8},{10,11... | collective-permute-start | bytes 393224 | tf_op jit(solution)/shard_map/ppermute | solution.py:154
  37.8 3.7 %collective-permute-done.9 = bf16[128,512]{1,0:T(8,128)(2,1)S(1)} collective-permute-done((bf16[128,512]{1,0:T(8,128)(2,1)S(1)}, bf16[128,512]{1,0:T(8,128)(2,1)S(1)}, u32[]{:S(2)}, u32[]{:S(2)}) %collective-permute-start.9) | collective-permute-done | bytes 131104 | tf_op jit(solution)/shard_map/ppermute | solution.py:154
  41.6 1.9 %collective-permute-done.6 = bf16[128,512]{1,0:T(8,128)(2,1)S(1)} collective-permute-done((bf16[128,512]{1,0:T(8,128)(2,1)S(1)}, bf16[128,512]{1,0:T(8,128)(2,1)S(1)}, u32[]{:S(2)}, u32[]{:S(2)}) %collective-permute-start.6) | collective-permute-done | bytes 131104 | tf_op jit(solution)/shard_map/ppermute | solution.py:154
  43.5 1.2 %collective-permute-start.11 = (bf16[64,512]{1,0:T(8,128)(2,1)S(1)}, bf16[64,512]{1,0:T(8,128)(2,1)S(1)}, u32[]{:S(2)}, u32[]{:S(2)}) collective-permute-start(bf16[64,512]{1,0:T(8,128)(2,1)S(1)} %get-tuple-element.51), channel_id=1, source_target_pairs={{0,8},{2,10},{4,12},{6,14},{8,0},{10,2},{12,4},{14,6},{1,9},{3,11}... | collective-permute-start | bytes 196616 | tf_op jit(solution)/shard_map/ppermute | solution.py:163
  44.8 1.4 %collective-permute-start.12 = (bf16[64,512]{1,0:T(8,128)(2,1)S(1)}, bf16[64,512]{1,0:T(8,128)(2,1)S(1)}, u32[]{:S(2)}, u32[]{:S(2)}) collective-permute-start(bf16[64,512]{1,0:T(8,128)(2,1)S(1)} %get-tuple-element.52.mark_ref), channel_id=1, source_target_pairs={{0,12},{2,14},{4,8},{6,10},{8,4},{10,6},{12,0},{14,2},{1,13},{3,15... | collective-permute-start | bytes 196616 | tf_op jit(solution)/shard_map/ppermute | solution.py:163
  46.2 2.2 %shard_map.96.up_ref = bf16[512,4096]{1,0:T(8,128)(2,1)S(1)} custom-call(bf16[64,512]{1,0:T(8,128)(2,1)S(1)} %get-tuple-element.52.mark_ref, bf16[512,4096]{1,0:T(8,128)(2,1)} %refs_0_.5), custom_call_target="tpu_custom_call" | custom-call | flops 1 | bytes 1 | tf_op jit(solution)/shard_map/pallas_call | solution.py:43
  48.4 2.6 %collective-permute-done.11.refs_2_ = bf16[64,512]{1,0:T(8,128)(2,1)S(1)} collective-permute-done((bf16[64,512]{1,0:T(8,128)(2,1)S(1)}, bf16[64,512]{1,0:T(8,128)(2,1)S(1)}, u32[]{:S(2)}, u32[]{:S(2)}) %collective-permute-start.11) | collective-permute-done | bytes 65568 | tf_op jit(solution)/shard_map/ppermute | solution.py:163
  51.5 1.5 %collective-permute-start.13 = (bf16[64,2048]{1,0:T(8,128)(2,1)S(1)}, bf16[64,2048]{1,0:T(8,128)(2,1)S(1)}, u32[]{:S(2)}, u32[]{:S(2)}) collective-permute-start(bf16[64,2048]{1,0:T(8,128)(2,1)S(1)} %get-tuple-element.50), channel_id=1, source_target_pairs={{0,1},{1,0},{2,3},{3,2},{4,5},{5,4},{6,7},{7,6},{8,9},{9,8},{10,11... | collective-permute-start | bytes 786440 | tf_op jit(solution)/shard_map/ppermute | solution.py:154
  53.5 4.8 %collective-permute-done.13 = bf16[64,2048]{1,0:T(8,128)(2,1)S(1)} collective-permute-done((bf16[64,2048]{1,0:T(8,128)(2,1)S(1)}, bf16[64,2048]{1,0:T(8,128)(2,1)S(1)}, u32[]{:S(2)}, u32[]{:S(2)}) %collective-permute-start.13) | collective-permute-done | bytes 262176 | tf_op jit(solution)/shard_map/ppermute | solution.py:154
  58.3 0.8 %add_convert_fusion = bf16[64,2048]{1,0:T(8,128)(2,1)} fusion(f32[64,2048]{1,0:T(8,128)S(1)} %shard_map.100, bf16[64,2048]{1,0:T(8,128)(2,1)S(1)} %collective-permute-done.13), kind=kLoop, calls=%fused_computation.1 | loop fusion | flops 393216 | bytes 1048576 | tf_op jit(solution)/shard_map/convert_element_type | solution.py:221
  (34 shorter events, 2.4 us)
Async XLA Ops:
  3.1 5.2 %copy-start.1 = (s32[2,32,16]{1,2,0:T(8,128)S(1)}, s32[2,32,16]{1,2,0:T(8,128)}, u32[]{:S(2)}) copy-start(s32[2,32,16]{1,2,0:T(8,128)} %param.10) | copy-start | bytes 12292
  3.1 5.2 %copy-start.2 = (s32[2,32,16]{1,2,0:T(8,128)S(1)}, s32[2,32,16]{1,2,0:T(8,128)}, u32[]{:S(2)}) copy-start(s32[2,32,16]{1,2,0:T(8,128)} %param.11) | copy-start | bytes 12292
  3.2 5.2 %copy-start.3 = (s32[32]{0:T(128)S(1)}, s32[32]{0:T(128)}, u32[]{:S(2)}) copy-start(s32[32]{0:T(128)} %param.12) | copy-start | bytes 388
  3.2 6.5 %collective-permute-start = (bf16[64,1024]{1,0:T(8,128)(2,1)S(1)}, bf16[64,1024]{1,0:T(8,128)(2,1)S(1)}, u32[]{:S(2)}, u32[]{:S(2)}) collective-permute-start(bf16[64,1024]{1,0:T(8,128)(2,1)S(1)} %convolution_convert_fusion.mark_ref), channel_id=1, source_target_pairs={{0,1},{1,0},{2,3},{3,2},{4,5},{5,4},{6,7},{7,6},{8,9},{9,8},{10,11... | collective-permute-start | bytes 393224 | tf_op jit(solution)/shard_map/ppermute | solution.py:154
  9.7 8.7 %collective-permute-start.3 = (bf16[64,1152]{1,0:T(8,128)(2,1)S(1)}, bf16[64,1152]{1,0:T(8,128)(2,1)S(1)}, u32[]{:S(2)}, u32[]{:S(2)}) collective-permute-start(bf16[64,1152]{1,0:T(8,128)(2,1)S(1)} %pad_maximum_fusion.mark_ref), channel_id=1, source_target_pairs={{0,12},{2,14},{4,8},{6,10},{8,4},{10,6},{12,0},{14,2},{1,13},{3,15... | collective-permute-start | bytes 442376 | tf_op jit(solution)/shard_map/ppermute | solution.py:163
  13.6 11.6 %collective-permute-start.2 = (bf16[64,1152]{1,0:T(8,128)(2,1)S(1)}, bf16[64,1152]{1,0:T(8,128)(2,1)S(1)}, u32[]{:S(2)}, u32[]{:S(2)}) collective-permute-start(bf16[64,1152]{1,0:T(8,128)(2,1)S(1)} %pad_maximum_fusion.mark_ref), channel_id=1, source_target_pairs={{0,8},{2,10},{4,12},{6,14},{8,0},{10,2},{12,4},{14,6},{1,9},{3,11}... | collective-permute-start | bytes 442376 | tf_op jit(solution)/shard_map/ppermute | solution.py:163
  13.6 11.6 %collective-permute-start.1 = (bf16[64,1152]{1,0:T(8,128)(2,1)S(1)}, bf16[64,1152]{1,0:T(8,128)(2,1)S(1)}, u32[]{:S(2)}, u32[]{:S(2)}) collective-permute-start(bf16[64,1152]{1,0:T(8,128)(2,1)S(1)} %pad_maximum_fusion.mark_ref), channel_id=1, source_target_pairs={{0,4},{2,6},{4,0},{6,2},{8,12},{10,14},{12,8},{14,10},{1,5},{3,7},... | collective-permute-start | bytes 442376 | tf_op jit(solution)/shard_map/ppermute | solution.py:163
  25.3 1.6 %collective-permute-start.7 = (bf16[128,1152]{1,0:T(8,128)(2,1)S(1)}, bf16[128,1152]{1,0:T(8,128)(2,1)S(1)}, u32[]{:S(2)}, u32[]{:S(2)}) collective-permute-start(bf16[128,1152]{1,0:T(8,128)(2,1)S(1)} %constant_dynamic-update-slice_fusion.2.own_ref), channel_id=1, source_target_pairs={{0,2},{2,0},{4,6},{6,4},{8,10},{10,8},{12,14},{14,12},{1,3},{3,1},... | collective-permute-start | bytes 884744 | tf_op jit(solution)/shard_map/ppermute | solution.py:159
  25.4 5.4 %collective-permute-start.4 = (bf16[128,1152]{1,0:T(8,128)(2,1)S(1)}, bf16[128,1152]{1,0:T(8,128)(2,1)S(1)}, u32[]{:S(2)}, u32[]{:S(2)}) collective-permute-start(bf16[128,1152]{1,0:T(8,128)(2,1)S(1)} %constant_dynamic-update-slice_fusion.own_ref), channel_id=1, source_target_pairs={{0,2},{2,0},{4,6},{6,4},{8,10},{10,8},{12,14},{14,12},{1,3},{3,1},... | collective-permute-start | bytes 884744 | tf_op jit(solution)/shard_map/ppermute | solution.py:159
  30.7 4.3 %collective-permute-start.8 = (bf16[128,1024]{1,0:T(8,128)(2,1)S(1)}, bf16[128,1024]{1,0:T(8,128)(2,1)S(1)}, u32[]{:S(2)}, u32[]{:S(2)}) collective-permute-start(bf16[128,1024]{1,0:T(8,128)(2,1)S(1)} %get-tuple-element.46), channel_id=1, source_target_pairs={{0,2},{2,0},{4,6},{6,4},{8,10},{10,8},{12,14},{14,12},{1,3},{3,1},... | collective-permute-start | bytes 786440 | tf_op jit(solution)/shard_map/ppermute | solution.py:159
  34.6 2.1 %collective-permute-start.5 = (bf16[128,1024]{1,0:T(8,128)(2,1)S(1)}, bf16[128,1024]{1,0:T(8,128)(2,1)S(1)}, u32[]{:S(2)}, u32[]{:S(2)}) collective-permute-start(bf16[128,1024]{1,0:T(8,128)(2,1)S(1)} %get-tuple-element.39), channel_id=1, source_target_pairs={{0,2},{2,0},{4,6},{6,4},{8,10},{10,8},{12,14},{14,12},{1,3},{3,1},... | collective-permute-start | bytes 786440 | tf_op jit(solution)/shard_map/ppermute | solution.py:159
  35.1 6.4 %collective-permute-start.9 = (bf16[128,512]{1,0:T(8,128)(2,1)S(1)}, bf16[128,512]{1,0:T(8,128)(2,1)S(1)}, u32[]{:S(2)}, u32[]{:S(2)}) collective-permute-start(bf16[128,512]{1,0:T(8,128)(2,1)S(1)} %get-tuple-element.48), channel_id=1, source_target_pairs={{0,1},{1,0},{2,3},{3,2},{4,5},{5,4},{6,7},{7,6},{8,9},{9,8},{10,11... | collective-permute-start | bytes 393224 | tf_op jit(solution)/shard_map/ppermute | solution.py:154
  36.7 6.8 %collective-permute-start.6 = (bf16[128,512]{1,0:T(8,128)(2,1)S(1)}, bf16[128,512]{1,0:T(8,128)(2,1)S(1)}, u32[]{:S(2)}, u32[]{:S(2)}) collective-permute-start(bf16[128,512]{1,0:T(8,128)(2,1)S(1)} %get-tuple-element.41), channel_id=1, source_target_pairs={{0,1},{1,0},{2,3},{3,2},{4,5},{5,4},{6,7},{7,6},{8,9},{9,8},{10,11... | collective-permute-start | bytes 393224 | tf_op jit(solution)/shard_map/ppermute | solution.py:154
  41.5 6.8 %collective-permute-start.10 = (bf16[64,512]{1,0:T(8,128)(2,1)S(1)}, bf16[64,512]{1,0:T(8,128)(2,1)S(1)}, u32[]{:S(2)}, u32[]{:S(2)}) collective-permute-start(bf16[64,512]{1,0:T(8,128)(2,1)S(1)} %get-tuple-element.53), channel_id=1, source_target_pairs={{0,4},{2,6},{4,0},{6,2},{8,12},{10,14},{12,8},{14,10},{1,5},{3,7},... | collective-permute-start | bytes 196616 | tf_op jit(solution)/shard_map/ppermute | solution.py:163
  43.5 7.4 %collective-permute-start.11 = (bf16[64,512]{1,0:T(8,128)(2,1)S(1)}, bf16[64,512]{1,0:T(8,128)(2,1)S(1)}, u32[]{:S(2)}, u32[]{:S(2)}) collective-permute-start(bf16[64,512]{1,0:T(8,128)(2,1)S(1)} %get-tuple-element.51), channel_id=1, source_target_pairs={{0,8},{2,10},{4,12},{6,14},{8,0},{10,2},{12,4},{14,6},{1,9},{3,11}... | collective-permute-start | bytes 196616 | tf_op jit(solution)/shard_map/ppermute | solution.py:163
  44.8 6.2 %collective-permute-start.12 = (bf16[64,512]{1,0:T(8,128)(2,1)S(1)}, bf16[64,512]{1,0:T(8,128)(2,1)S(1)}, u32[]{:S(2)}, u32[]{:S(2)}) collective-permute-start(bf16[64,512]{1,0:T(8,128)(2,1)S(1)} %get-tuple-element.52.mark_ref), channel_id=1, source_target_pairs={{0,12},{2,14},{4,8},{6,10},{8,4},{10,6},{12,0},{14,2},{1,13},{3,15... | collective-permute-start | bytes 196616 | tf_op jit(solution)/shard_map/ppermute | solution.py:163
  48.4 4.7 %copy-start = (bf16[2,32,2048]{2,1,0:T(8,128)(2,1)S(1)}, bf16[2,32,2048]{2,1,0:T(8,128)(2,1)}, u32[]{:S(2)}) copy-start(bf16[2,32,2048]{2,1,0:T(8,128)(2,1)} %param.9) | copy-start | bytes 786436
  51.5 6.8 %collective-permute-start.13 = (bf16[64,2048]{1,0:T(8,128)(2,1)S(1)}, bf16[64,2048]{1,0:T(8,128)(2,1)S(1)}, u32[]{:S(2)}, u32[]{:S(2)}) collective-permute-start(bf16[64,2048]{1,0:T(8,128)(2,1)S(1)} %get-tuple-element.50), channel_id=1, source_target_pairs={{0,1},{1,0},{2,3},{3,2},{4,5},{5,4},{6,7},{7,6},{8,9},{9,8},{10,11... | collective-permute-start | bytes 786440 | tf_op jit(solution)/shard_map/ppermute | solution.py:154

commit v3 on v2

--- a/solution.py
+++ b/solution.py
@@ -52,42 +52,74 @@
     )(mark, *held)
 
 
-def route_kernel(ids_ref, route_ref, slot_ref, weight_ref, norm_ref):
+def route_kernel(ids_ref, route_ref, slot_ref, packed_ref, norm_ref):
     steps, top_count, rows = ids_ref.shape
-    slots, padded = slot_ref.shape[1], weight_ref.shape[1]
+    slots, group = slot_ref.shape[1], packed_ref.shape[0]
     every = lax.broadcasted_iota(jnp.int32, (slots, rows), 0)
-    move = lax.broadcasted_iota(jnp.int32, (padded, slots), 0) == slot_ref[...]
+    move = lax.broadcasted_iota(jnp.int32, (LANES, slots), 0) == slot_ref[...]
     move = jnp.where(move, 1.0, 0.0).astype(jnp.bfloat16)
+    packed = None
     for s in range(steps):
         ids, route = ids_ref[s], route_ref[s].astype(jnp.float32)
         by_expert = jnp.zeros((slots, rows), jnp.float32)
         for k in range(top_count):
             by_expert = by_expert + jnp.where(every == ids[k : k + 1], route[k : k + 1], 0.0)
-        by_slot = jnp.dot(move, by_expert.astype(jnp.bfloat16), preferred_element_type=jnp.float32)
-        at = pl.ds(s * rows, rows)
-        weight_ref[at, :] = by_slot.T.astype(jnp.bfloat16)
+        by_slot = jnp.dot(move, by_expert.astype(jnp.bfloat16), preferred_element_type=jnp.float32).T
+        for g in range(rows // group):
+            at = (s * rows // group + g) * slots
+            part = by_slot[g * group : (g + 1) * group]
+            part = pltpu.roll(part, at, 1) if at else part
+            packed = part if packed is None else packed + part
         norm = jnp.broadcast_to(jnp.sum(route, axis=0, keepdims=True), (norm_ref.shape[1], rows))
-        norm_ref[at, :] = norm.T
-
-
-def expert_kernel(own_ref, pair_ref, gate_ref, up_ref, down_ref, own_out_ref, pair_out_ref):
+        norm_ref[pl.ds(s * rows, rows), :] = norm.T
+    packed_ref[...] = packed.astype(packed_ref.dtype)
+
+
+def pack_kernel(*refs):
+    *terms, packed_ref, out_ref = refs
+    rows, width = terms[0].shape
+    for c in range(width // LANES):
+        at = slice(c * LANES, (c + 1) * LANES)
+        total = terms[0][:, at].astype(jnp.float32)
+        for term in terms[1:]:
+            total = total + term[:, at].astype(jnp.float32)
+        out_ref[c * rows : (c + 1) * rows, :] = total.astype(out_ref.dtype)
+    out_ref[width // LANES * rows :, :] = packed_ref[...]
+
+
+def expert_kernel(rows, slots, own_ref, pair_ref, gate_ref, up_ref, down_ref, own_out_ref, pair_out_ref):
     local_count, width = gate_ref.shape[0], gate_ref.shape[1]
-    both = jnp.concatenate([own_ref[...], pair_ref[...]], axis=0)
-    rows, weights = both[:, :width], both[:, width:].astype(jnp.float32)
-    lanes = lax.broadcasted_iota(jnp.int32, weights.shape, 1)
+    columns, group = width // LANES, rows * slots // LANES
+    size = columns * rows + group
+    latent, packed = [], []
+    for ref in (own_ref, pair_ref):
+        for b in range(0, ref.shape[0], size):
+            parts = [ref[b + c * rows : b + (c + 1) * rows, :] for c in range(columns)]
+            latent.append(jnp.concatenate(parts, axis=1))
+            packed.append(ref[b + columns * rows : b + size, :])
+    both, packed = jnp.concatenate(latent, axis=0), jnp.concatenate(packed, axis=0)
     first = lax.axis_index("expert") * local_count
-    total = None
+    lane = lax.broadcasted_iota(jnp.int32, (LANES, LANES), 0)
+    column = lax.broadcasted_iota(jnp.int32, (LANES, LANES), 1)
+    spread = []
+    for g in range(LANES // slots):
+        take = jnp.where(lane == column + (first + g * slots), 1.0, 0.0).astype(jnp.bfloat16)
+        spread.append(jnp.dot(packed, take, preferred_element_type=jnp.float32))
+    weights = jnp.concatenate(
+        [part[b : b + group] for b in range(0, packed.shape[0], group) for part in spread], axis=0
+    )
+    hidden = []
     for j in range(local_count):
-        gate_act = jnp.dot(rows, gate_ref[j], preferred_element_type=jnp.float32)
-        up_act = jnp.dot(rows, up_ref[j], preferred_element_type=jnp.float32)
-        weight = jnp.sum(jnp.where(lanes == first + j, weights, 0.0), axis=1, keepdims=True)
-        hidden = (gate_act / (1.0 + jnp.exp(-gate_act)) * up_act * weight).astype(jnp.bfloat16)
-        term = jnp.dot(hidden, down_ref[j], preferred_element_type=jnp.float32)
-        total = term if total is None else total + term
-    total = total.astype(jnp.bfloat16)
-    half = own_out_ref.shape[0]
-    own_out_ref[...] = total[:half]
-    pair_out_ref[...] = total[half:]
+        gate_act = jnp.dot(both, gate_ref[j], preferred_element_type=jnp.float32)
+        up_act = jnp.dot(both, up_ref[j], preferred_element_type=jnp.float32)
+        silu = gate_act / (1.0 + jnp.exp(-gate_act))
+        hidden.append((silu * up_act * weights[:, j : j + 1]).astype(jnp.bfloat16))
+    hidden = jnp.concatenate(hidden, axis=1)
+    down = down_ref[...].reshape(hidden.shape[1], width)
+    total = jnp.dot(hidden, down, preferred_element_type=jnp.float32).astype(jnp.bfloat16)
+    half_rows = own_out_ref.shape[0]
+    own_out_ref[...] = total[:half_rows]
+    pair_out_ref[...] = total[half_rows:]
 
 
 def fold_kernel(tensor_count, *refs):
@@ -166,25 +198,26 @@
 
     inputs = tokens.reshape(rows, features)
     slots = expert_slot.shape[0]
-    weights, norm = call(
+    packed, norm = call(
         route_kernel,
-        [((rows, -(-slots // LANES) * LANES), jnp.bfloat16), ((rows, LANES), jnp.float32)],
+        [((rows * slots // LANES, LANES), jnp.bfloat16), ((rows, LANES), jnp.float32)],
         expert_ids.transpose(0, 2, 1),
         route_weights.transpose(0, 2, 1),
         expert_slot.reshape(1, slots),
     )
     partial = jnp.dot(inputs, latent_down, preferred_element_type=jnp.float32).astype(jnp.bfloat16)
-    latent = add(partial, *[across(partial, s) for s in range(1, tensor_count)])
+    terms = [partial] + [across(partial, s) for s in range(1, tensor_count)]
     (gate_proj,) = fetch(partial, gate_proj)
-    latent, weights, gate_proj = lax.optimization_barrier((latent, weights, gate_proj))
-    payload = jnp.concatenate([latent.astype(jnp.bfloat16), weights], axis=1)
+    terms, packed, gate_proj = lax.optimization_barrier((terms, packed, gate_proj))
+    size = rows * latent_width // LANES + packed.shape[0]
+    (payload,) = call(pack_kernel, [((size, LANES), jnp.bfloat16)], *terms, packed)
     blocks = [payload] + [far_swap(payload, s) for s in range(1, far)]
     up_proj, down_proj = fetch(payload, up_proj, down_proj)
-    *blocks, up_proj, down_proj = lax.optimization_barrier((*blocks, up_proj, down_proj))
 
     def apply(own, other):
-        shape = ((own.shape[0], latent_width), jnp.bfloat16)
-        return call(expert_kernel, [shape] * 2, own, other, gate_proj, up_proj, down_proj)
+        shape = ((own.shape[0] // size * rows, latent_width), jnp.bfloat16)
+        kernel = functools.partial(expert_kernel, rows, slots)
+        return call(kernel, [shape] * 2, own, other, gate_proj, up_proj, down_proj)
 
     def fold(*terms):
         shape = ((terms[0].shape[0], block), jnp.bfloat16)
@@ -196,14 +229,29 @@
     def join(own, other):
         return fold(own, swap(other)) if pair == 2 else fold(jnp.concatenate([own, other], axis=0))
 
-    cut = far // 2
-    pieces = []
-    for part in (blocks[cut:], blocks[:cut]) if cut else (blocks,):
-        own = jnp.concatenate(part, axis=0)
-        held, *away = join(*apply(*halves(own)))
+    def spread(held, *away):
         arrived = [across(x, s + 1) for s, x in enumerate(away)]
         sums = add(held, *arrived).astype(jnp.bfloat16)
-        pieces = [sums[i : i + rows] for i in range(0, sums.shape[0], rows)] + pieces
+        return [sums[i : i + rows] for i in range(0, sums.shape[0], rows)]
+
+    def run(part):
+        return join(*apply(*halves(jnp.concatenate(part, axis=0))))
+
+    cut = max(far // 2, 1)
+    first = run(blocks[:1])
+    *first, up_proj, down_proj, blocks[1:] = lax.optimization_barrier(
+        (*first, up_proj, down_proj, blocks[1:])
+    )
+    pieces = spread(*first)
+    if far > cut:
+        last = run(blocks[cut:])
+        if cut > 1:
+            *last, blocks[1] = lax.optimization_barrier((*last, blocks[1]))
+            middle = run(blocks[1:cut])
+            last = spread(*last)
+            pieces += spread(*middle) + last
+        else:
+            pieces += spread(*last)
     (latent_up,) = fetch(pieces[-1], latent_up)
     pieces = [pieces[0]] + [far_swap(pieces[s], s, back=True) for s in range(1, far)]
 

time: 59.2 us -> 56.1 us (0.948)
  waiting for transfers between devices: 22.4 us -> 18.3 us
  starting transfers between devices: 15.7 us -> 16.6 us
    ppermute x6, waiting for transfers between devices: 10.1 us -> 6.03 us  [far_swap(): lax.ppermute(x, 'expert', [(i, i ^ s * pair) for i in range(expert_axis)])]
    ppermute x4 -> x5, waiting for transfers between devices: 11.3 us -> 8.02 us  [across(): lax.ppermute(x, 'tensor', [(i, (i + s) % tensor_count) for i in range(ten...]
    ppermute x4 -> x6, waiting for transfers between devices: 1 us -> 4.27 us  [swap(): return lax.ppermute(x, 'expert', [(i, i ^ 1) for i in range(expert_axis)])]
    ppermute x6, starting transfers between devices: 7.25 us -> 8.03 us  [far_swap(): lax.ppermute(x, 'expert', [(i, i ^ s * pair) for i in range(expert_axis)])]
    ppermute x4 -> x5, starting transfers between devices: 7.2 us -> 7.88 us  [across(): lax.ppermute(x, 'tensor', [(i, (i + s) % tensor_count) for i in range(ten...]
    ppermute x4 -> x6, starting transfers between devices: 1.27 us -> 0.69 us  [swap(): return lax.ppermute(x, 'expert', [(i, i ^ 1) for i in range(expert_axis)])]
    pallas_call x7 -> x10, Pallas kernels: 8.79 us -> 8.89 us  [call(): pl.pallas_call(kernel, in_specs=whole(len(operands)), out_specs=whole(len...]
  transfers between devices with their start and end apart: 14 -> 17, of which waited for: 8 -> 10; matrix products, arithmetic and copies ran while one was open for 0% -> 0% of each run, Pallas kernels for 27% -> 23%
where the time goes in v3:
time: 56.1 us; the launch traced here: 55.9 us
  waiting for transfers between devices  18.3 us (33%)
  Pallas kernels  16.8 us (30%)
  starting transfers between devices  16.6 us (30%)
  matrix products  3.12 us (6%)
  other arithmetic  0.82 us (1%)
    pallas_call x10, Pallas kernels, call(): pl.pallas_call(kernel, in_specs=whole(len(operands)), out_specs=whole(len...  8.89 us
    ppermute x6, starting transfers between devices, far_swap(): lax.ppermute(x, 'expert', [(i, i ^ s * pair) for i in range(expert_axis)])  8.03 us
    ppermute x5, waiting for transfers between devices, across(): lax.ppermute(x, 'tensor', [(i, (i + s) % tensor_count) for i in range(ten...  8.02 us
    ppermute x5, starting transfers between devices, across(): lax.ppermute(x, 'tensor', [(i, (i + s) % tensor_count) for i in range(ten...  7.88 us
    pallas_call x3, Pallas kernels, fetch(): pl.pallas_call(fetch_kernel, in_specs=[pl.BlockSpec(memory_space=pl.ANY)]...  7.88 us
    ppermute x6, waiting for transfers between devices, far_swap(): lax.ppermute(x, 'expert', [(i, i ^ s * pair) for i in range(expert_axis)])  6.03 us
    ppermute x6, waiting for transfers between devices, swap(): return lax.ppermute(x, 'expert', [(i, i ^ 1) for i in range(expert_axis)])  4.27 us
    dot_general x1, matrix products, shards(): jnp.dot(inputs, latent_down, preferred_element_type=jnp.float32)  3.12 us
  transfers between devices with their start and end apart: 17, of which 10 were waited for; matrix products, arithmetic and copies ran while one was open for 0% of the time, Pallas kernels for 23%

profile of v3, /device:TPU:0, one launch (start us, length us, event | category | flops | bytes accessed | tf_op | source)
XLA Modules:
  0.0 55.9 jit_solution(3019367792983596003)
XLA Ops:
  0.0 3.1 %convolution_convert_fusion.mark_ref.refs_0_ = bf16[64,1024]{1,0:T(8,128)(2,1)S(1)} fusion(bf16[64,2048]{1,0:T(8,128)(2,1)} %bitcast.7, bf16[2048,1024]{1,0:T(8,128)(2,1)} %param.13), kind=kOutput, calls=%fused_computation | convolution fusion | flops 268500992 | bytes 4587520 | tf_op jit(solution)/shard_map/dot_general | solution.py:208
  3.2 3.0 %collective-permute-start = (bf16[64,1024]{1,0:T(8,128)(2,1)S(1)}, bf16[64,1024]{1,0:T(8,128)(2,1)S(1)}, u32[]{:S(2)}, u32[]{:S(2)}) collective-permute-start(bf16[64,1024]{1,0:T(8,128)(2,1)S(1)} %convolution_convert_fusion.mark_ref.refs_0_), channel_id=1, source_target_pairs={{0,1},{1,0},{2,3},{3,2},{4,5},{5,4},{6,7},{7,6},{8,9},{9,8},{10,11... | collective-permute-start | bytes 393224 | tf_op jit(solution)/shard_map/ppermute | solution.py:186
  6.2 2.2 %shard_map.92.gate_ref = bf16[4,1024,512]{2,1,0:T(8,128)(2,1)S(1)} custom-call(bf16[64,1024]{1,0:T(8,128)(2,1)S(1)} %convolution_convert_fusion.mark_ref.refs_0_, bf16[4,1024,512]{2,1,0:T(8,128)(2,1)} %refs_0_.3), custom_call_target="tpu_custom_call" | custom-call | flops 1 | bytes 1 | tf_op jit(solution)/shard_map/pallas_call | solution.py:43
  8.7 0.9 %collective-permute-done.refs_1_ = bf16[64,1024]{1,0:T(8,128)(2,1)S(1)} collective-permute-done((bf16[64,1024]{1,0:T(8,128)(2,1)S(1)}, bf16[64,1024]{1,0:T(8,128)(2,1)S(1)}, u32[]{:S(2)}, u32[]{:S(2)}) %collective-permute-start) | collective-permute-done | bytes 131104 | tf_op jit(solution)/shard_map/ppermute | solution.py:186
  9.8 3.9 %collective-permute-start.5 = (bf16[528,128]{1,0:T(8,128)(2,1)S(1)}, bf16[528,128]{1,0:T(8,128)(2,1)S(1)}, u32[]{:S(2)}, u32[]{:S(2)}) collective-permute-start(bf16[528,128]{1,0:T(8,128)(2,1)S(1)} %shard_map.93.mark_ref.own_ref), channel_id=1, source_target_pairs={{0,12},{2,14},{4,8},{6,10},{8,4},{10,6},{12,0},{14,2},{1,13},{3,15... | collective-permute-start | bytes 405512 | tf_op jit(solution)/shard_map/ppermute | solution.py:195
  13.7 0.6 %collective-permute-start.3 = (bf16[528,128]{1,0:T(8,128)(2,1)S(1)}, bf16[528,128]{1,0:T(8,128)(2,1)S(1)}, u32[]{:S(2)}, u32[]{:S(2)}) collective-permute-start(bf16[528,128]{1,0:T(8,128)(2,1)S(1)} %shard_map.93.mark_ref.own_ref), channel_id=1, source_target_pairs={{0,4},{2,6},{4,0},{6,2},{8,12},{10,14},{12,8},{14,10},{1,5},{3,7},... | collective-permute-start | bytes 405512 | tf_op jit(solution)/shard_map/ppermute | solution.py:195
  14.3 3.5 %shard_map.94 = (bf16[4,1024,512]{2,1,0:T(8,128)(2,1)S(1)}, bf16[4,512,1024]{2,1,0:T(8,128)(2,1)S(1)}) custom-call(bf16[528,128]{1,0:T(8,128)(2,1)S(1)} %shard_map.93.mark_ref.own_ref, bf16[4,1024,512]{2,1,0:T(8,128)(2,1)} %refs_0_.4, bf16[4,512,1024]{2,1,0:T(8,128)(2,1)} %refs_1_.1), custom_call_target="tpu_custom_call" | custom-call | flops 1 | bytes 1 | tf_op jit(solution)/shard_map/pallas_call | solution.py:43
  17.8 1.9 %shard_map.95 = (bf16[64,1024]{1,0:T(8,128)(2,1)S(1)}, bf16[64,1024]{1,0:T(8,128)(2,1)S(1)}) custom-call(bf16[528,128]{1,0:T(8,128)(2,1)S(1)} %shard_map.93.mark_ref.own_ref, bf16[528,128]{1,0:T(8,128)(2,1)S(1)} %collective-permute-done.1.pair_ref, bf16[4,1024,512]{2,1,0:T(8,128)(2,1)S(1)} %shard_map.92.gate_ref, ...), custom_call_target="tpu_custom_call" | custom-call | flops 1 | bytes 1 | tf_op jit(solution)/shard_map/pallas_call | solution.py:21
  19.8 1.3 %collective-permute-done.2.refs_1_ = bf16[64,1024]{1,0:T(8,128)(2,1)S(1)} collective-permute-done((bf16[64,1024]{1,0:T(8,128)(2,1)S(1)}, bf16[64,1024]{1,0:T(8,128)(2,1)S(1)}, u32[]{:S(2)}, u32[]{:S(2)}) %collective-permute-start.2) | collective-permute-done | bytes 131104 | tf_op jit(solution)/shard_map/ppermute | solution.py:191
  21.2 4.5 %collective-permute-done.4 = bf16[528,128]{1,0:T(8,128)(2,1)S(1)} collective-permute-done((bf16[528,128]{1,0:T(8,128)(2,1)S(1)}, bf16[528,128]{1,0:T(8,128)(2,1)S(1)}, u32[]{:S(2)}, u32[]{:S(2)}) %collective-permute-start.4) | collective-permute-done | bytes 135200 | tf_op jit(solution)/shard_map/ppermute | solution.py:195
  25.9 1.5 %collective-permute-done.6.pair_ref = bf16[1056,128]{1,0:T(8,128)(2,1)S(1)} collective-permute-done((bf16[1056,128]{1,0:T(8,128)(2,1)S(1)}, bf16[1056,128]{1,0:T(8,128)(2,1)S(1)}, u32[]{:S(2)}, u32[]{:S(2)}) %collective-permute-start.6) | collective-permute-done | bytes 270368 | tf_op jit(solution)/shard_map/ppermute | solution.py:191
  27.4 3.6 %shard_map.97 = (bf16[128,1024]{1,0:T(8,128)(2,1)S(1)}, bf16[128,1024]{1,0:T(8,128)(2,1)S(1)}) custom-call(bf16[1056,128]{1,0:T(8,128)(2,1)S(1)} %constant_dynamic-update-slice_fusion.own_ref, bf16[1056,128]{1,0:T(8,128)(2,1)S(1)} %collective-permute-done.6.pair_ref, bf16[4,1024,512]{2,1,0:T(8,128)(2,1)S(1)} %shard_map.92.gate_ref, ...), custom_call_target="tpu_custom_call" | custom-call | flops 1 | bytes 1 | tf_op jit(solution)/shard_map/pallas_call | solution.py:21
  31.2 1.4 %collective-permute-done.7.refs_1_ = bf16[128,1024]{1,0:T(8,128)(2,1)S(1)} collective-permute-done((bf16[128,1024]{1,0:T(8,128)(2,1)S(1)}, bf16[128,1024]{1,0:T(8,128)(2,1)S(1)}, u32[]{:S(2)}, u32[]{:S(2)}) %collective-permute-start.7) | collective-permute-done | bytes 262176 | tf_op jit(solution)/shard_map/ppermute | solution.py:191
  32.8 1.5 %collective-permute-start.8 = (bf16[128,512]{1,0:T(8,128)(2,1)S(1)}, bf16[128,512]{1,0:T(8,128)(2,1)S(1)}, u32[]{:S(2)}, u32[]{:S(2)}) collective-permute-start(bf16[128,512]{1,0:T(8,128)(2,1)S(1)} %get-tuple-element.58), channel_id=1, source_target_pairs={{0,1},{1,0},{2,3},{3,2},{4,5},{5,4},{6,7},{7,6},{8,9},{9,8},{10,11... | collective-permute-start | bytes 393224 | tf_op jit(solution)/shard_map/ppermute | solution.py:186
  34.9 1.9 %shard_map.100 = (bf16[64,1024]{1,0:T(8,128)(2,1)S(1)}, bf16[64,1024]{1,0:T(8,128)(2,1)S(1)}) custom-call(bf16[528,128]{1,0:T(8,128)(2,1)S(1)} %collective-permute-done.3.own_ref, bf16[528,128]{1,0:T(8,128)(2,1)S(1)} %collective-permute-done.10.pair_ref, bf16[4,1024,512]{2,1,0:T(8,128)(2,1)S(1)} %shard_map.92.gate_ref, ...), custom_call_target="tpu_custom_call" | custom-call | flops 1 | bytes 1 | tf_op jit(solution)/shard_map/pallas_call | solution.py:21
  36.9 2.3 %collective-permute-done.8 = bf16[128,512]{1,0:T(8,128)(2,1)S(1)} collective-permute-done((bf16[128,512]{1,0:T(8,128)(2,1)S(1)}, bf16[128,512]{1,0:T(8,128)(2,1)S(1)}, u32[]{:S(2)}, u32[]{:S(2)}) %collective-permute-start.8) | collective-permute-done | bytes 131104 | tf_op jit(solution)/shard_map/ppermute | solution.py:186
  39.3 1.6 %collective-permute-start.12 = (bf16[64,512]{1,0:T(8,128)(2,1)S(1)}, bf16[64,512]{1,0:T(8,128)(2,1)S(1)}, u32[]{:S(2)}, u32[]{:S(2)}) collective-permute-start(bf16[64,512]{1,0:T(8,128)(2,1)S(1)} %get-tuple-element.66), channel_id=1, source_target_pairs={{0,1},{1,0},{2,3},{3,2},{4,5},{5,4},{6,7},{7,6},{8,9},{9,8},{10,11... | collective-permute-start | bytes 196616 | tf_op jit(solution)/shard_map/ppermute | solution.py:186
  40.9 2.5 %collective-permute-start.15 = (bf16[64,512]{1,0:T(8,128)(2,1)S(1)}, bf16[64,512]{1,0:T(8,128)(2,1)S(1)}, u32[]{:S(2)}, u32[]{:S(2)}) collective-permute-start(bf16[64,512]{1,0:T(8,128)(2,1)S(1)} %get-tuple-element.70.mark_ref), channel_id=1, source_target_pairs={{0,12},{2,14},{4,8},{6,10},{8,4},{10,6},{12,0},{14,2},{1,13},{3,15... | collective-permute-start | bytes 196616 | tf_op jit(solution)/shard_map/ppermute | solution.py:195
  43.6 0.9 %collective-permute-start.13 = (bf16[64,512]{1,0:T(8,128)(2,1)S(1)}, bf16[64,512]{1,0:T(8,128)(2,1)S(1)}, u32[]{:S(2)}, u32[]{:S(2)}) collective-permute-start(bf16[64,512]{1,0:T(8,128)(2,1)S(1)} %add_convert_fusion.2), channel_id=1, source_target_pairs={{0,4},{2,6},{4,0},{6,2},{8,12},{10,14},{12,8},{14,10},{1,5},{3,7},... | collective-permute-start | bytes 196616 | tf_op jit(solution)/shard_map/ppermute | solution.py:195
  44.5 2.2 %shard_map.99.up_ref = bf16[512,4096]{1,0:T(8,128)(2,1)S(1)} custom-call(bf16[64,512]{1,0:T(8,128)(2,1)S(1)} %get-tuple-element.70.mark_ref, bf16[512,4096]{1,0:T(8,128)(2,1)} %refs_0_.5), custom_call_target="tpu_custom_call" | custom-call | flops 1 | bytes 1 | tf_op jit(solution)/shard_map/pallas_call | solution.py:43
  46.7 1.1 %collective-permute-done.14.refs_2_ = bf16[64,512]{1,0:T(8,128)(2,1)S(1)} collective-permute-done((bf16[64,512]{1,0:T(8,128)(2,1)S(1)}, bf16[64,512]{1,0:T(8,128)(2,1)S(1)}, u32[]{:S(2)}, u32[]{:S(2)}) %collective-permute-start.14) | collective-permute-done | bytes 65568 | tf_op jit(solution)/shard_map/ppermute | solution.py:195
  48.8 1.3 %collective-permute-start.16 = (bf16[64,2048]{1,0:T(8,128)(2,1)S(1)}, bf16[64,2048]{1,0:T(8,128)(2,1)S(1)}, u32[]{:S(2)}, u32[]{:S(2)}) collective-permute-start(bf16[64,2048]{1,0:T(8,128)(2,1)S(1)} %get-tuple-element.68), channel_id=1, source_target_pairs={{0,1},{1,0},{2,3},{3,2},{4,5},{5,4},{6,7},{7,6},{8,9},{9,8},{10,11... | collective-permute-start | bytes 786440 | tf_op jit(solution)/shard_map/ppermute | solution.py:186
  50.5 4.7 %collective-permute-done.16 = bf16[64,2048]{1,0:T(8,128)(2,1)S(1)} collective-permute-done((bf16[64,2048]{1,0:T(8,128)(2,1)S(1)}, bf16[64,2048]{1,0:T(8,128)(2,1)S(1)}, u32[]{:S(2)}, u32[]{:S(2)}) %collective-permute-start.16) | collective-permute-done | bytes 262176 | tf_op jit(solution)/shard_map/ppermute | solution.py:186
  55.2 0.8 %add_convert_fusion = bf16[64,2048]{1,0:T(8,128)(2,1)} fusion(f32[64,2048]{1,0:T(8,128)S(1)} %shard_map.103, bf16[64,2048]{1,0:T(8,128)(2,1)S(1)} %collective-permute-done.16), kind=kLoop, calls=%fused_computation.1 | loop fusion | flops 393216 | bytes 1048576 | tf_op jit(solution)/shard_map/convert_element_type | solution.py:269
  (39 shorter events, 3.5 us)
Async XLA Ops:
  3.1 5.2 %copy-start.1 = (s32[2,32,16]{1,2,0:T(8,128)S(1)}, s32[2,32,16]{1,2,0:T(8,128)}, u32[]{:S(2)}) copy-start(s32[2,32,16]{1,2,0:T(8,128)} %param.10) | copy-start | bytes 12292
  3.1 5.2 %copy-start.2 = (s32[2,32,16]{1,2,0:T(8,128)S(1)}, s32[2,32,16]{1,2,0:T(8,128)}, u32[]{:S(2)}) copy-start(s32[2,32,16]{1,2,0:T(8,128)} %param.11) | copy-start | bytes 12292
  3.2 5.2 %copy-start.3 = (s32[32]{0:T(128)S(1)}, s32[32]{0:T(128)}, u32[]{:S(2)}) copy-start(s32[32]{0:T(128)} %param.12) | copy-start | bytes 388
  3.2 6.5 %collective-permute-start = (bf16[64,1024]{1,0:T(8,128)(2,1)S(1)}, bf16[64,1024]{1,0:T(8,128)(2,1)S(1)}, u32[]{:S(2)}, u32[]{:S(2)}) collective-permute-start(bf16[64,1024]{1,0:T(8,128)(2,1)S(1)} %convolution_convert_fusion.mark_ref.refs_0_), channel_id=1, source_target_pairs={{0,1},{1,0},{2,3},{3,2},{4,5},{5,4},{6,7},{7,6},{8,9},{9,8},{10,11... | collective-permute-start | bytes 393224 | tf_op jit(solution)/shard_map/ppermute | solution.py:186
  9.7 8.1 %collective-permute-start.1 = (bf16[528,128]{1,0:T(8,128)(2,1)S(1)}, bf16[528,128]{1,0:T(8,128)(2,1)S(1)}, u32[]{:S(2)}, u32[]{:S(2)}) collective-permute-start(bf16[528,128]{1,0:T(8,128)(2,1)S(1)} %shard_map.93.mark_ref.own_ref), channel_id=1, source_target_pairs={{0,2},{2,0},{4,6},{6,4},{8,10},{10,8},{12,14},{14,12},{1,3},{3,1},... | collective-permute-start | bytes 405512 | tf_op jit(solution)/shard_map/ppermute | solution.py:191
  9.8 11.4 %collective-permute-start.5 = (bf16[528,128]{1,0:T(8,128)(2,1)S(1)}, bf16[528,128]{1,0:T(8,128)(2,1)S(1)}, u32[]{:S(2)}, u32[]{:S(2)}) collective-permute-start(bf16[528,128]{1,0:T(8,128)(2,1)S(1)} %shard_map.93.mark_ref.own_ref), channel_id=1, source_target_pairs={{0,12},{2,14},{4,8},{6,10},{8,4},{10,6},{12,0},{14,2},{1,13},{3,15... | collective-permute-start | bytes 405512 | tf_op jit(solution)/shard_map/ppermute | solution.py:195
  13.7 12.0 %collective-permute-start.4 = (bf16[528,128]{1,0:T(8,128)(2,1)S(1)}, bf16[528,128]{1,0:T(8,128)(2,1)S(1)}, u32[]{:S(2)}, u32[]{:S(2)}) collective-permute-start(bf16[528,128]{1,0:T(8,128)(2,1)S(1)} %shard_map.93.mark_ref.own_ref), channel_id=1, source_target_pairs={{0,8},{2,10},{4,12},{6,14},{8,0},{10,2},{12,4},{14,6},{1,9},{3,11}... | collective-permute-start | bytes 405512 | tf_op jit(solution)/shard_map/ppermute | solution.py:195
  13.7 12.0 %collective-permute-start.3 = (bf16[528,128]{1,0:T(8,128)(2,1)S(1)}, bf16[528,128]{1,0:T(8,128)(2,1)S(1)}, u32[]{:S(2)}, u32[]{:S(2)}) collective-permute-start(bf16[528,128]{1,0:T(8,128)(2,1)S(1)} %shard_map.93.mark_ref.own_ref), channel_id=1, source_target_pairs={{0,4},{2,6},{4,0},{6,2},{8,12},{10,14},{12,8},{14,10},{1,5},{3,7},... | collective-permute-start | bytes 405512 | tf_op jit(solution)/shard_map/ppermute | solution.py:195
  19.8 1.4 %collective-permute-start.2 = (bf16[64,1024]{1,0:T(8,128)(2,1)S(1)}, bf16[64,1024]{1,0:T(8,128)(2,1)S(1)}, u32[]{:S(2)}, u32[]{:S(2)}) collective-permute-start(bf16[64,1024]{1,0:T(8,128)(2,1)S(1)} %get-tuple-element.45), channel_id=1, source_target_pairs={{0,2},{2,0},{4,6},{6,4},{8,10},{10,8},{12,14},{14,12},{1,3},{3,1},... | collective-permute-start | bytes 393224 | tf_op jit(solution)/shard_map/ppermute | solution.py:191
  25.8 1.6 %collective-permute-start.6 = (bf16[1056,128]{1,0:T(8,128)(2,1)S(1)}, bf16[1056,128]{1,0:T(8,128)(2,1)S(1)}, u32[]{:S(2)}, u32[]{:S(2)}) collective-permute-start(bf16[1056,128]{1,0:T(8,128)(2,1)S(1)} %constant_dynamic-update-slice_fusion.own_ref), channel_id=1, source_target_pairs={{0,2},{2,0},{4,6},{6,4},{8,10},{10,8},{12,14},{14,12},{1,3},{3,1},... | collective-permute-start | bytes 811016 | tf_op jit(solution)/shard_map/ppermute | solution.py:191
  31.0 1.6 %collective-permute-start.7 = (bf16[128,1024]{1,0:T(8,128)(2,1)S(1)}, bf16[128,1024]{1,0:T(8,128)(2,1)S(1)}, u32[]{:S(2)}, u32[]{:S(2)}) collective-permute-start(bf16[128,1024]{1,0:T(8,128)(2,1)S(1)} %get-tuple-element.53), channel_id=1, source_target_pairs={{0,2},{2,0},{4,6},{6,4},{8,10},{10,8},{12,14},{14,12},{1,3},{3,1},... | collective-permute-start | bytes 786440 | tf_op jit(solution)/shard_map/ppermute | solution.py:191
  32.6 2.2 %collective-permute-start.10 = (bf16[528,128]{1,0:T(8,128)(2,1)S(1)}, bf16[528,128]{1,0:T(8,128)(2,1)S(1)}, u32[]{:S(2)}, u32[]{:S(2)}) collective-permute-start(bf16[528,128]{1,0:T(8,128)(2,1)S(1)} %collective-permute-done.3.own_ref), channel_id=1, source_target_pairs={{0,2},{2,0},{4,6},{6,4},{8,10},{10,8},{12,14},{14,12},{1,3},{3,1},... | collective-permute-start | bytes 405512 | tf_op jit(solution)/shard_map/ppermute | solution.py:191
  32.8 6.3 %collective-permute-start.8 = (bf16[128,512]{1,0:T(8,128)(2,1)S(1)}, bf16[128,512]{1,0:T(8,128)(2,1)S(1)}, u32[]{:S(2)}, u32[]{:S(2)}) collective-permute-start(bf16[128,512]{1,0:T(8,128)(2,1)S(1)} %get-tuple-element.58), channel_id=1, source_target_pairs={{0,1},{1,0},{2,3},{3,2},{4,5},{5,4},{6,7},{7,6},{8,9},{9,8},{10,11... | collective-permute-start | bytes 393224 | tf_op jit(solution)/shard_map/ppermute | solution.py:186
  34.3 10.1 %collective-permute-start.9 = (bf16[64,512]{1,0:T(8,128)(2,1)S(1)}, bf16[64,512]{1,0:T(8,128)(2,1)S(1)}, u32[]{:S(2)}, u32[]{:S(2)}) collective-permute-start(bf16[64,512]{1,0:T(8,128)(2,1)S(1)} %get-tuple-element.61), channel_id=1, source_target_pairs={{0,1},{1,0},{2,3},{3,2},{4,5},{5,4},{6,7},{7,6},{8,9},{9,8},{10,11... | collective-permute-start | bytes 196616 | tf_op jit(solution)/shard_map/ppermute | solution.py:186
  36.8 2.4 %collective-permute-start.11 = (bf16[64,1024]{1,0:T(8,128)(2,1)S(1)}, bf16[64,1024]{1,0:T(8,128)(2,1)S(1)}, u32[]{:S(2)}, u32[]{:S(2)}) collective-permute-start(bf16[64,1024]{1,0:T(8,128)(2,1)S(1)} %get-tuple-element.64), channel_id=1, source_target_pairs={{0,2},{2,0},{4,6},{6,4},{8,10},{10,8},{12,14},{14,12},{1,3},{3,1},... | collective-permute-start | bytes 393224 | tf_op jit(solution)/shard_map/ppermute | solution.py:191
  39.3 4.3 %collective-permute-start.12 = (bf16[64,512]{1,0:T(8,128)(2,1)S(1)}, bf16[64,512]{1,0:T(8,128)(2,1)S(1)}, u32[]{:S(2)}, u32[]{:S(2)}) collective-permute-start(bf16[64,512]{1,0:T(8,128)(2,1)S(1)} %get-tuple-element.66), channel_id=1, source_target_pairs={{0,1},{1,0},{2,3},{3,2},{4,5},{5,4},{6,7},{7,6},{8,9},{9,8},{10,11... | collective-permute-start | bytes 196616 | tf_op jit(solution)/shard_map/ppermute | solution.py:186
  40.8 7.0 %collective-permute-start.14 = (bf16[64,512]{1,0:T(8,128)(2,1)S(1)}, bf16[64,512]{1,0:T(8,128)(2,1)S(1)}, u32[]{:S(2)}, u32[]{:S(2)}) collective-permute-start(bf16[64,512]{1,0:T(8,128)(2,1)S(1)} %get-tuple-element.69), channel_id=1, source_target_pairs={{0,8},{2,10},{4,12},{6,14},{8,0},{10,2},{12,4},{14,6},{1,9},{3,11}... | collective-permute-start | bytes 196616 | tf_op jit(solution)/shard_map/ppermute | solution.py:195
  40.9 6.9 %collective-permute-start.15 = (bf16[64,512]{1,0:T(8,128)(2,1)S(1)}, bf16[64,512]{1,0:T(8,128)(2,1)S(1)}, u32[]{:S(2)}, u32[]{:S(2)}) collective-permute-start(bf16[64,512]{1,0:T(8,128)(2,1)S(1)} %get-tuple-element.70.mark_ref), channel_id=1, source_target_pairs={{0,12},{2,14},{4,8},{6,10},{8,4},{10,6},{12,0},{14,2},{1,13},{3,15... | collective-permute-start | bytes 196616 | tf_op jit(solution)/shard_map/ppermute | solution.py:195
  43.6 4.6 %collective-permute-start.13 = (bf16[64,512]{1,0:T(8,128)(2,1)S(1)}, bf16[64,512]{1,0:T(8,128)(2,1)S(1)}, u32[]{:S(2)}, u32[]{:S(2)}) collective-permute-start(bf16[64,512]{1,0:T(8,128)(2,1)S(1)} %add_convert_fusion.2), channel_id=1, source_target_pairs={{0,4},{2,6},{4,0},{6,2},{8,12},{10,14},{12,8},{14,10},{1,5},{3,7},... | collective-permute-start | bytes 196616 | tf_op jit(solution)/shard_map/ppermute | solution.py:195
  46.7 3.3 %copy-start = (bf16[2,32,2048]{2,1,0:T(8,128)(2,1)S(1)}, bf16[2,32,2048]{2,1,0:T(8,128)(2,1)}, u32[]{:S(2)}) copy-start(bf16[2,32,2048]{2,1,0:T(8,128)(2,1)} %param.9) | copy-start | bytes 786436
  48.8 6.4 %collective-permute-start.16 = (bf16[64,2048]{1,0:T(8,128)(2,1)S(1)}, bf16[64,2048]{1,0:T(8,128)(2,1)S(1)}, u32[]{:S(2)}, u32[]{:S(2)}) collective-permute-start(bf16[64,2048]{1,0:T(8,128)(2,1)S(1)} %get-tuple-element.68), channel_id=1, source_target_pairs={{0,1},{1,0},{2,3},{3,2},{4,5},{5,4},{6,7},{7,6},{8,9},{9,8},{10,11... | collective-permute-start | bytes 786440 | tf_op jit(solution)/shard_map/ppermute | solution.py:186

commit v4 on v3

--- a/solution.py
+++ b/solution.py
@@ -87,12 +87,13 @@
     out_ref[width // LANES * rows :, :] = packed_ref[...]
 
 
-def expert_kernel(rows, slots, own_ref, pair_ref, gate_ref, up_ref, down_ref, own_out_ref, pair_out_ref):
+def expert_kernel(rows, slots, gate_ref, up_ref, down_ref, *refs):
+    payloads, outs = refs[: len(refs) // 2], refs[len(refs) // 2 :]
     local_count, width = gate_ref.shape[0], gate_ref.shape[1]
     columns, group = width // LANES, rows * slots // LANES
     size = columns * rows + group
     latent, packed = [], []
-    for ref in (own_ref, pair_ref):
+    for ref in payloads:
         for b in range(0, ref.shape[0], size):
             parts = [ref[b + c * rows : b + (c + 1) * rows, :] for c in range(columns)]
             latent.append(jnp.concatenate(parts, axis=1))
@@ -117,9 +118,10 @@
     hidden = jnp.concatenate(hidden, axis=1)
     down = down_ref[...].reshape(hidden.shape[1], width)
     total = jnp.dot(hidden, down, preferred_element_type=jnp.float32).astype(jnp.bfloat16)
-    half_rows = own_out_ref.shape[0]
-    own_out_ref[...] = total[:half_rows]
-    pair_out_ref[...] = total[half_rows:]
+    at = 0
+    for out in outs:
+        out[...] = total[at : at + out.shape[0]]
+        at += out.shape[0]
 
 
 def fold_kernel(tensor_count, *refs):
@@ -214,10 +216,10 @@
     blocks = [payload] + [far_swap(payload, s) for s in range(1, far)]
     up_proj, down_proj = fetch(payload, up_proj, down_proj)
 
-    def apply(own, other):
-        shape = ((own.shape[0] // size * rows, latent_width), jnp.bfloat16)
+    def apply(*payloads):
+        shapes = [((x.shape[0] // size * rows, latent_width), jnp.bfloat16) for x in payloads]
         kernel = functools.partial(expert_kernel, rows, slots)
-        return call(kernel, [shape] * 2, own, other, gate_proj, up_proj, down_proj)
+        return call(kernel, shapes, gate_proj, up_proj, down_proj, *payloads)
 
     def fold(*terms):
         shape = ((terms[0].shape[0], block), jnp.bfloat16)
@@ -244,14 +246,17 @@
     )
     pieces = spread(*first)
     if far > cut:
-        last = run(blocks[cut:])
+        own, other = halves(jnp.concatenate(blocks[cut:], axis=0))
+        last = [*apply(own), *apply(other)]
         if cut > 1:
-            *last, blocks[1] = lax.optimization_barrier((*last, blocks[1]))
-            middle = run(blocks[1:cut])
-            last = spread(*last)
-            pieces += spread(*middle) + last
+            middle = halves(jnp.concatenate(blocks[1:cut], axis=0))
+            last, middle = lax.optimization_barrier((last, middle))
+            middle = apply(*middle)
+            last = join(*last)
+            last, middle = lax.optimization_barrier((last, middle))
+            pieces += spread(*join(*middle)) + spread(*last)
         else:
-            pieces += spread(*last)
+            pieces += spread(*join(*last))
     (latent_up,) = fetch(pieces[-1], latent_up)
     pieces = [pieces[0]] + [far_swap(pieces[s], s, back=True) for s in range(1, far)]
 

time: 56.1 us -> 54.6 us (0.973)
  waiting for transfers between devices: 18.3 us -> 15.4 us
  starting transfers between devices: 16.6 us -> 17.7 us
    ppermute x6, waiting for transfers between devices: 4.27 us -> 1.35 us  [swap(): return lax.ppermute(x, 'expert', [(i, i ^ 1) for i in range(expert_axis)])]
    ppermute x6, starting transfers between devices: 0.69 us -> 1.35 us  [swap(): return lax.ppermute(x, 'expert', [(i, i ^ 1) for i in range(expert_axis)])]
    pallas_call x10 -> x11, Pallas kernels: 8.89 us -> 9.16 us  [call(): pl.pallas_call(kernel, in_specs=whole(len(operands)), out_specs=whole(len...]
  transfers between devices with their start and end apart: 17 -> 17, of which waited for: 10 -> 7; matrix products, arithmetic and copies ran while one was open for 0% -> 0% of each run, Pallas kernels for 23% -> 30%
where the time goes in v4:
time: 54.6 us; the launch traced here: 54.4 us
  starting transfers between devices  17.7 us (32%)
  Pallas kernels  17 us (31%)
  waiting for transfers between devices  15.4 us (28%)
  matrix products  3.12 us (6%)
  other arithmetic  0.82 us (2%)
    pallas_call x11, Pallas kernels, call(): pl.pallas_call(kernel, in_specs=whole(len(operands)), out_specs=whole(len...  9.16 us
    ppermute x6, starting transfers between devices, far_swap(): lax.ppermute(x, 'expert', [(i, i ^ s * pair) for i in range(expert_axis)])  8.17 us
    ppermute x5, starting transfers between devices, across(): lax.ppermute(x, 'tensor', [(i, (i + s) % tensor_count) for i in range(ten...  8.14 us
    ppermute x5, waiting for transfers between devices, across(): lax.ppermute(x, 'tensor', [(i, (i + s) % tensor_count) for i in range(ten...  8.05 us
    pallas_call x3, Pallas kernels, fetch(): pl.pallas_call(fetch_kernel, in_specs=[pl.BlockSpec(memory_space=pl.ANY)]...  7.88 us
    ppermute x6, waiting for transfers between devices, far_swap(): lax.ppermute(x, 'expert', [(i, i ^ s * pair) for i in range(expert_axis)])  6 us
    dot_general x1, matrix products, shards(): jnp.dot(inputs, latent_down, preferred_element_type=jnp.float32)  3.12 us
    ppermute x6, starting transfers between devices, swap(): return lax.ppermute(x, 'expert', [(i, i ^ 1) for i in range(expert_axis)])  1.35 us
  transfers between devices with their start and end apart: 17, of which 7 were waited for; matrix products, arithmetic and copies ran while one was open for 0% of the time, Pallas kernels for 30%

profile of v4, /device:TPU:0, one launch (start us, length us, event | category | flops | bytes accessed | tf_op | source)
XLA Modules:
  0.0 54.4 jit_solution(5370567205906356721)
XLA Ops:
  0.0 3.1 %convolution_convert_fusion.mark_ref.refs_0_ = bf16[64,1024]{1,0:T(8,128)(2,1)S(1)} fusion(bf16[64,2048]{1,0:T(8,128)(2,1)} %bitcast.7, bf16[2048,1024]{1,0:T(8,128)(2,1)} %param.13), kind=kOutput, calls=%fused_computation | convolution fusion | flops 268500992 | bytes 4587520 | tf_op jit(solution)/shard_map/dot_general | solution.py:210
  3.2 3.0 %collective-permute-start = (bf16[64,1024]{1,0:T(8,128)(2,1)S(1)}, bf16[64,1024]{1,0:T(8,128)(2,1)S(1)}, u32[]{:S(2)}, u32[]{:S(2)}) collective-permute-start(bf16[64,1024]{1,0:T(8,128)(2,1)S(1)} %convolution_convert_fusion.mark_ref.refs_0_), channel_id=1, source_target_pairs={{0,1},{1,0},{2,3},{3,2},{4,5},{5,4},{6,7},{7,6},{8,9},{9,8},{10,11... | collective-permute-start | bytes 393224 | tf_op jit(solution)/shard_map/ppermute | solution.py:188
  6.2 2.2 %shard_map.92.gate_ref = bf16[4,1024,512]{2,1,0:T(8,128)(2,1)S(1)} custom-call(bf16[64,1024]{1,0:T(8,128)(2,1)S(1)} %convolution_convert_fusion.mark_ref.refs_0_, bf16[4,1024,512]{2,1,0:T(8,128)(2,1)} %refs_0_.3), custom_call_target="tpu_custom_call" | custom-call | flops 1 | bytes 1 | tf_op jit(solution)/shard_map/pallas_call | solution.py:43
  8.7 0.9 %collective-permute-done.refs_1_ = bf16[64,1024]{1,0:T(8,128)(2,1)S(1)} collective-permute-done((bf16[64,1024]{1,0:T(8,128)(2,1)S(1)}, bf16[64,1024]{1,0:T(8,128)(2,1)S(1)}, u32[]{:S(2)}, u32[]{:S(2)}) %collective-permute-start) | collective-permute-done | bytes 131104 | tf_op jit(solution)/shard_map/ppermute | solution.py:188
  9.8 3.9 %collective-permute-start.5 = (bf16[528,128]{1,0:T(8,128)(2,1)S(1)}, bf16[528,128]{1,0:T(8,128)(2,1)S(1)}, u32[]{:S(2)}, u32[]{:S(2)}) collective-permute-start(bf16[528,128]{1,0:T(8,128)(2,1)S(1)} %shard_map.93.mark_ref.refs_0_), channel_id=1, source_target_pairs={{0,12},{2,14},{4,8},{6,10},{8,4},{10,6},{12,0},{14,2},{1,13},{3,15... | collective-permute-start | bytes 405512 | tf_op jit(solution)/shard_map/ppermute | solution.py:197
  13.7 0.6 %collective-permute-start.3 = (bf16[528,128]{1,0:T(8,128)(2,1)S(1)}, bf16[528,128]{1,0:T(8,128)(2,1)S(1)}, u32[]{:S(2)}, u32[]{:S(2)}) collective-permute-start(bf16[528,128]{1,0:T(8,128)(2,1)S(1)} %shard_map.93.mark_ref.refs_0_), channel_id=1, source_target_pairs={{0,4},{2,6},{4,0},{6,2},{8,12},{10,14},{12,8},{14,10},{1,5},{3,7},... | collective-permute-start | bytes 405512 | tf_op jit(solution)/shard_map/ppermute | solution.py:197
  14.3 3.5 %shard_map.94 = (bf16[4,1024,512]{2,1,0:T(8,128)(2,1)S(1)}, bf16[4,512,1024]{2,1,0:T(8,128)(2,1)S(1)}) custom-call(bf16[528,128]{1,0:T(8,128)(2,1)S(1)} %shard_map.93.mark_ref.refs_0_, bf16[4,1024,512]{2,1,0:T(8,128)(2,1)} %refs_0_.4, bf16[4,512,1024]{2,1,0:T(8,128)(2,1)} %refs_1_.1), custom_call_target="tpu_custom_call" | custom-call | flops 1 | bytes 1 | tf_op jit(solution)/shard_map/pallas_call | solution.py:43
  17.8 1.9 %shard_map.95 = (bf16[64,1024]{1,0:T(8,128)(2,1)S(1)}, bf16[64,1024]{1,0:T(8,128)(2,1)S(1)}) custom-call(bf16[4,1024,512]{2,1,0:T(8,128)(2,1)S(1)} %shard_map.92.gate_ref, bf16[4,1024,512]{2,1,0:T(8,128)(2,1)S(1)} %get-tuple-element.51.up_ref, bf16[4,512,1024]{2,1,0:T(8,128)(2,1)S(1)} %get-tuple-element.52.down_ref, ...), custom_call_target="tpu_custom_call" | custom-call | flops 1 | bytes 1 | tf_op jit(solution)/shard_map/pallas_call | solution.py:21
  19.8 1.3 %collective-permute-done.2.refs_1_ = bf16[64,1024]{1,0:T(8,128)(2,1)S(1)} collective-permute-done((bf16[64,1024]{1,0:T(8,128)(2,1)S(1)}, bf16[64,1024]{1,0:T(8,128)(2,1)S(1)}, u32[]{:S(2)}, u32[]{:S(2)}) %collective-permute-start.2) | collective-permute-done | bytes 131104 | tf_op jit(solution)/shard_map/ppermute | solution.py:193
  21.2 4.5 %collective-permute-done.4 = bf16[528,128]{1,0:T(8,128)(2,1)S(1)} collective-permute-done((bf16[528,128]{1,0:T(8,128)(2,1)S(1)}, bf16[528,128]{1,0:T(8,128)(2,1)S(1)}, u32[]{:S(2)}, u32[]{:S(2)}) %collective-permute-start.4) | collective-permute-done | bytes 135200 | tf_op jit(solution)/shard_map/ppermute | solution.py:197
  26.4 1.9 %shard_map.97.refs_0_ = bf16[128,1024]{1,0:T(8,128)(2,1)S(1)} custom-call(bf16[4,1024,512]{2,1,0:T(8,128)(2,1)S(1)} %shard_map.92.gate_ref, bf16[4,1024,512]{2,1,0:T(8,128)(2,1)S(1)} %get-tuple-element.51.up_ref, bf16[4,512,1024]{2,1,0:T(8,128)(2,1)S(1)} %get-tuple-element.52.down_ref, bf16[1056,128]{1,0:T(8,128)(2,1)S(1)} %constant_dynamic-update-slice_fusion.refs_0_), custom_call_target="tpu_custom_call" | custom-call | flops 1 | bytes 1 | tf_op jit(solution)/shard_map/pallas_call | solution.py:21
  28.3 1.9 %shard_map.98 = bf16[128,1024]{1,0:T(8,128)(2,1)S(1)} custom-call(bf16[4,1024,512]{2,1,0:T(8,128)(2,1)S(1)} %shard_map.92.gate_ref, bf16[4,1024,512]{2,1,0:T(8,128)(2,1)S(1)} %get-tuple-element.51.up_ref, bf16[4,512,1024]{2,1,0:T(8,128)(2,1)S(1)} %get-tuple-element.52.down_ref, bf16[1056,128]{1,0:T(8,128)(2,1)S(1)} %collective-permute-done.6.refs_0_), custom_call_target="tpu_custom_call" | custom-call | flops 1 | bytes 1 | tf_op jit(solution)/shard_map/pallas_call | solution.py:21
  30.3 1.9 %shard_map.100 = (bf16[64,1024]{1,0:T(8,128)(2,1)S(1)}, bf16[64,1024]{1,0:T(8,128)(2,1)S(1)}) custom-call(bf16[4,1024,512]{2,1,0:T(8,128)(2,1)S(1)} %shard_map.92.gate_ref, bf16[4,1024,512]{2,1,0:T(8,128)(2,1)S(1)} %get-tuple-element.51.up_ref, bf16[4,512,1024]{2,1,0:T(8,128)(2,1)S(1)} %get-tuple-element.52.down_ref, ...), custom_call_target="tpu_custom_call" | custom-call | flops 1 | bytes 1 | tf_op jit(solution)/shard_map/pallas_call | solution.py:21
  32.9 1.5 %collective-permute-start.9 = (bf16[128,512]{1,0:T(8,128)(2,1)S(1)}, bf16[128,512]{1,0:T(8,128)(2,1)S(1)}, u32[]{:S(2)}, u32[]{:S(2)}) collective-permute-start(bf16[128,512]{1,0:T(8,128)(2,1)S(1)} %get-tuple-element.65), channel_id=1, source_target_pairs={{0,1},{1,0},{2,3},{3,2},{4,5},{5,4},{6,7},{7,6},{8,9},{9,8},{10,11... | collective-permute-start | bytes 393224 | tf_op jit(solution)/shard_map/ppermute | solution.py:188
  34.9 1.6 %collective-permute-start.12 = (bf16[64,512]{1,0:T(8,128)(2,1)S(1)}, bf16[64,512]{1,0:T(8,128)(2,1)S(1)}, u32[]{:S(2)}, u32[]{:S(2)}) collective-permute-start(bf16[64,512]{1,0:T(8,128)(2,1)S(1)} %get-tuple-element.72), channel_id=1, source_target_pairs={{0,1},{1,0},{2,3},{3,2},{4,5},{5,4},{6,7},{7,6},{8,9},{9,8},{10,11... | collective-permute-start | bytes 196616 | tf_op jit(solution)/shard_map/ppermute | solution.py:188
  36.5 2.7 %collective-permute-done.9 = bf16[128,512]{1,0:T(8,128)(2,1)S(1)} collective-permute-done((bf16[128,512]{1,0:T(8,128)(2,1)S(1)}, bf16[128,512]{1,0:T(8,128)(2,1)S(1)}, u32[]{:S(2)}, u32[]{:S(2)}) %collective-permute-start.9) | collective-permute-done | bytes 131104 | tf_op jit(solution)/shard_map/ppermute | solution.py:188
  39.4 2.5 %collective-permute-start.15 = (bf16[64,512]{1,0:T(8,128)(2,1)S(1)}, bf16[64,512]{1,0:T(8,128)(2,1)S(1)}, u32[]{:S(2)}, u32[]{:S(2)}) collective-permute-start(bf16[64,512]{1,0:T(8,128)(2,1)S(1)} %get-tuple-element.76.mark_ref), channel_id=1, source_target_pairs={{0,12},{2,14},{4,8},{6,10},{8,4},{10,6},{12,0},{14,2},{1,13},{3,15... | collective-permute-start | bytes 196616 | tf_op jit(solution)/shard_map/ppermute | solution.py:197
  41.9 1.0 %collective-permute-start.13 = (bf16[64,512]{1,0:T(8,128)(2,1)S(1)}, bf16[64,512]{1,0:T(8,128)(2,1)S(1)}, u32[]{:S(2)}, u32[]{:S(2)}) collective-permute-start(bf16[64,512]{1,0:T(8,128)(2,1)S(1)} %add_convert_fusion.2), channel_id=1, source_target_pairs={{0,4},{2,6},{4,0},{6,2},{8,12},{10,14},{12,8},{14,10},{1,5},{3,7},... | collective-permute-start | bytes 196616 | tf_op jit(solution)/shard_map/ppermute | solution.py:197
  43.0 2.2 %shard_map.101.up_ref = bf16[512,4096]{1,0:T(8,128)(2,1)S(1)} custom-call(bf16[64,512]{1,0:T(8,128)(2,1)S(1)} %get-tuple-element.76.mark_ref, bf16[512,4096]{1,0:T(8,128)(2,1)} %refs_0_.5), custom_call_target="tpu_custom_call" | custom-call | flops 1 | bytes 1 | tf_op jit(solution)/shard_map/pallas_call | solution.py:43
  45.2 0.9 %collective-permute-done.14.refs_2_ = bf16[64,512]{1,0:T(8,128)(2,1)S(1)} collective-permute-done((bf16[64,512]{1,0:T(8,128)(2,1)S(1)}, bf16[64,512]{1,0:T(8,128)(2,1)S(1)}, u32[]{:S(2)}, u32[]{:S(2)}) %collective-permute-start.14) | collective-permute-done | bytes 65568 | tf_op jit(solution)/shard_map/ppermute | solution.py:197
  46.1 0.6 %collective-permute-done.13.refs_1_ = bf16[64,512]{1,0:T(8,128)(2,1)S(1)} collective-permute-done((bf16[64,512]{1,0:T(8,128)(2,1)S(1)}, bf16[64,512]{1,0:T(8,128)(2,1)S(1)}, u32[]{:S(2)}, u32[]{:S(2)}) %collective-permute-start.13) | collective-permute-done | bytes 65568 | tf_op jit(solution)/shard_map/ppermute | solution.py:197
  47.2 1.6 %collective-permute-start.16 = (bf16[64,2048]{1,0:T(8,128)(2,1)S(1)}, bf16[64,2048]{1,0:T(8,128)(2,1)S(1)}, u32[]{:S(2)}, u32[]{:S(2)}) collective-permute-start(bf16[64,2048]{1,0:T(8,128)(2,1)S(1)} %get-tuple-element.74), channel_id=1, source_target_pairs={{0,1},{1,0},{2,3},{3,2},{4,5},{5,4},{6,7},{7,6},{8,9},{9,8},{10,11... | collective-permute-start | bytes 786440 | tf_op jit(solution)/shard_map/ppermute | solution.py:188
  49.2 4.4 %collective-permute-done.16 = bf16[64,2048]{1,0:T(8,128)(2,1)S(1)} collective-permute-done((bf16[64,2048]{1,0:T(8,128)(2,1)S(1)}, bf16[64,2048]{1,0:T(8,128)(2,1)S(1)}, u32[]{:S(2)}, u32[]{:S(2)}) %collective-permute-start.16) | collective-permute-done | bytes 262176 | tf_op jit(solution)/shard_map/ppermute | solution.py:188
  53.6 0.8 %add_convert_fusion = bf16[64,2048]{1,0:T(8,128)(2,1)} fusion(f32[64,2048]{1,0:T(8,128)S(1)} %shard_map.104, bf16[64,2048]{1,0:T(8,128)(2,1)S(1)} %collective-permute-done.16), kind=kLoop, calls=%fused_computation.1 | loop fusion | flops 393216 | bytes 1048576 | tf_op jit(solution)/shard_map/convert_element_type | solution.py:274
  (40 shorter events, 3.6 us)
Async XLA Ops:
  3.1 5.2 %copy-start.1 = (s32[2,32,16]{1,2,0:T(8,128)S(1)}, s32[2,32,16]{1,2,0:T(8,128)}, u32[]{:S(2)}) copy-start(s32[2,32,16]{1,2,0:T(8,128)} %param.10) | copy-start | bytes 12292
  3.1 5.2 %copy-start.2 = (s32[2,32,16]{1,2,0:T(8,128)S(1)}, s32[2,32,16]{1,2,0:T(8,128)}, u32[]{:S(2)}) copy-start(s32[2,32,16]{1,2,0:T(8,128)} %param.11) | copy-start | bytes 12292
  3.2 5.2 %copy-start.3 = (s32[32]{0:T(128)S(1)}, s32[32]{0:T(128)}, u32[]{:S(2)}) copy-start(s32[32]{0:T(128)} %param.12) | copy-start | bytes 388
  3.2 6.5 %collective-permute-start = (bf16[64,1024]{1,0:T(8,128)(2,1)S(1)}, bf16[64,1024]{1,0:T(8,128)(2,1)S(1)}, u32[]{:S(2)}, u32[]{:S(2)}) collective-permute-start(bf16[64,1024]{1,0:T(8,128)(2,1)S(1)} %convolution_convert_fusion.mark_ref.refs_0_), channel_id=1, source_target_pairs={{0,1},{1,0},{2,3},{3,2},{4,5},{5,4},{6,7},{7,6},{8,9},{9,8},{10,11... | collective-permute-start | bytes 393224 | tf_op jit(solution)/shard_map/ppermute | solution.py:188
  9.7 8.1 %collective-permute-start.1 = (bf16[528,128]{1,0:T(8,128)(2,1)S(1)}, bf16[528,128]{1,0:T(8,128)(2,1)S(1)}, u32[]{:S(2)}, u32[]{:S(2)}) collective-permute-start(bf16[528,128]{1,0:T(8,128)(2,1)S(1)} %shard_map.93.mark_ref.refs_0_), channel_id=1, source_target_pairs={{0,2},{2,0},{4,6},{6,4},{8,10},{10,8},{12,14},{14,12},{1,3},{3,1},... | collective-permute-start | bytes 405512 | tf_op jit(solution)/shard_map/ppermute | solution.py:193
  9.8 11.4 %collective-permute-start.5 = (bf16[528,128]{1,0:T(8,128)(2,1)S(1)}, bf16[528,128]{1,0:T(8,128)(2,1)S(1)}, u32[]{:S(2)}, u32[]{:S(2)}) collective-permute-start(bf16[528,128]{1,0:T(8,128)(2,1)S(1)} %shard_map.93.mark_ref.refs_0_), channel_id=1, source_target_pairs={{0,12},{2,14},{4,8},{6,10},{8,4},{10,6},{12,0},{14,2},{1,13},{3,15... | collective-permute-start | bytes 405512 | tf_op jit(solution)/shard_map/ppermute | solution.py:197
  13.7 12.0 %collective-permute-start.4 = (bf16[528,128]{1,0:T(8,128)(2,1)S(1)}, bf16[528,128]{1,0:T(8,128)(2,1)S(1)}, u32[]{:S(2)}, u32[]{:S(2)}) collective-permute-start(bf16[528,128]{1,0:T(8,128)(2,1)S(1)} %shard_map.93.mark_ref.refs_0_), channel_id=1, source_target_pairs={{0,8},{2,10},{4,12},{6,14},{8,0},{10,2},{12,4},{14,6},{1,9},{3,11}... | collective-permute-start | bytes 405512 | tf_op jit(solution)/shard_map/ppermute | solution.py:197
  13.7 12.0 %collective-permute-start.3 = (bf16[528,128]{1,0:T(8,128)(2,1)S(1)}, bf16[528,128]{1,0:T(8,128)(2,1)S(1)}, u32[]{:S(2)}, u32[]{:S(2)}) collective-permute-start(bf16[528,128]{1,0:T(8,128)(2,1)S(1)} %shard_map.93.mark_ref.refs_0_), channel_id=1, source_target_pairs={{0,4},{2,6},{4,0},{6,2},{8,12},{10,14},{12,8},{14,10},{1,5},{3,7},... | collective-permute-start | bytes 405512 | tf_op jit(solution)/shard_map/ppermute | solution.py:197
  19.8 1.4 %collective-permute-start.2 = (bf16[64,1024]{1,0:T(8,128)(2,1)S(1)}, bf16[64,1024]{1,0:T(8,128)(2,1)S(1)}, u32[]{:S(2)}, u32[]{:S(2)}) collective-permute-start(bf16[64,1024]{1,0:T(8,128)(2,1)S(1)} %get-tuple-element.48), channel_id=1, source_target_pairs={{0,2},{2,0},{4,6},{6,4},{8,10},{10,8},{12,14},{14,12},{1,3},{3,1},... | collective-permute-start | bytes 393224 | tf_op jit(solution)/shard_map/ppermute | solution.py:193
  25.8 2.5 %collective-permute-start.6 = (bf16[1056,128]{1,0:T(8,128)(2,1)S(1)}, bf16[1056,128]{1,0:T(8,128)(2,1)S(1)}, u32[]{:S(2)}, u32[]{:S(2)}) collective-permute-start(bf16[1056,128]{1,0:T(8,128)(2,1)S(1)} %constant_dynamic-update-slice_fusion.refs_0_), channel_id=1, source_target_pairs={{0,2},{2,0},{4,6},{6,4},{8,10},{10,8},{12,14},{14,12},{1,3},{3,1},... | collective-permute-start | bytes 811016 | tf_op jit(solution)/shard_map/ppermute | solution.py:193
  25.9 4.3 %collective-permute-start.7 = (bf16[528,128]{1,0:T(8,128)(2,1)S(1)}, bf16[528,128]{1,0:T(8,128)(2,1)S(1)}, u32[]{:S(2)}, u32[]{:S(2)}) collective-permute-start(bf16[528,128]{1,0:T(8,128)(2,1)S(1)} %collective-permute-done.3.refs_0_), channel_id=1, source_target_pairs={{0,2},{2,0},{4,6},{6,4},{8,10},{10,8},{12,14},{14,12},{1,3},{3,1},... | collective-permute-start | bytes 405512 | tf_op jit(solution)/shard_map/ppermute | solution.py:193
  30.2 2.1 %collective-permute-start.8 = (bf16[128,1024]{1,0:T(8,128)(2,1)S(1)}, bf16[128,1024]{1,0:T(8,128)(2,1)S(1)}, u32[]{:S(2)}, u32[]{:S(2)}) collective-permute-start(bf16[128,1024]{1,0:T(8,128)(2,1)S(1)} %shard_map.98), channel_id=1, source_target_pairs={{0,2},{2,0},{4,6},{6,4},{8,10},{10,8},{12,14},{14,12},{1,3},{3,1},... | collective-permute-start | bytes 786440 | tf_op jit(solution)/shard_map/ppermute | solution.py:193
  32.4 2.5 %collective-permute-start.11 = (bf16[64,1024]{1,0:T(8,128)(2,1)S(1)}, bf16[64,1024]{1,0:T(8,128)(2,1)S(1)}, u32[]{:S(2)}, u32[]{:S(2)}) collective-permute-start(bf16[64,1024]{1,0:T(8,128)(2,1)S(1)} %get-tuple-element.70), channel_id=1, source_target_pairs={{0,2},{2,0},{4,6},{6,4},{8,10},{10,8},{12,14},{14,12},{1,3},{3,1},... | collective-permute-start | bytes 393224 | tf_op jit(solution)/shard_map/ppermute | solution.py:193
  32.9 6.4 %collective-permute-start.9 = (bf16[128,512]{1,0:T(8,128)(2,1)S(1)}, bf16[128,512]{1,0:T(8,128)(2,1)S(1)}, u32[]{:S(2)}, u32[]{:S(2)}) collective-permute-start(bf16[128,512]{1,0:T(8,128)(2,1)S(1)} %get-tuple-element.65), channel_id=1, source_target_pairs={{0,1},{1,0},{2,3},{3,2},{4,5},{5,4},{6,7},{7,6},{8,9},{9,8},{10,11... | collective-permute-start | bytes 393224 | tf_op jit(solution)/shard_map/ppermute | solution.py:188
  34.4 8.6 %collective-permute-start.10 = (bf16[64,512]{1,0:T(8,128)(2,1)S(1)}, bf16[64,512]{1,0:T(8,128)(2,1)S(1)}, u32[]{:S(2)}, u32[]{:S(2)}) collective-permute-start(bf16[64,512]{1,0:T(8,128)(2,1)S(1)} %get-tuple-element.68), channel_id=1, source_target_pairs={{0,1},{1,0},{2,3},{3,2},{4,5},{5,4},{6,7},{7,6},{8,9},{9,8},{10,11... | collective-permute-start | bytes 196616 | tf_op jit(solution)/shard_map/ppermute | solution.py:188
  34.9 7.0 %collective-permute-start.12 = (bf16[64,512]{1,0:T(8,128)(2,1)S(1)}, bf16[64,512]{1,0:T(8,128)(2,1)S(1)}, u32[]{:S(2)}, u32[]{:S(2)}) collective-permute-start(bf16[64,512]{1,0:T(8,128)(2,1)S(1)} %get-tuple-element.72), channel_id=1, source_target_pairs={{0,1},{1,0},{2,3},{3,2},{4,5},{5,4},{6,7},{7,6},{8,9},{9,8},{10,11... | collective-permute-start | bytes 196616 | tf_op jit(solution)/shard_map/ppermute | solution.py:188
  39.3 6.8 %collective-permute-start.14 = (bf16[64,512]{1,0:T(8,128)(2,1)S(1)}, bf16[64,512]{1,0:T(8,128)(2,1)S(1)}, u32[]{:S(2)}, u32[]{:S(2)}) collective-permute-start(bf16[64,512]{1,0:T(8,128)(2,1)S(1)} %get-tuple-element.75), channel_id=1, source_target_pairs={{0,8},{2,10},{4,12},{6,14},{8,0},{10,2},{12,4},{14,6},{1,9},{3,11}... | collective-permute-start | bytes 196616 | tf_op jit(solution)/shard_map/ppermute | solution.py:197
  39.4 6.7 %collective-permute-start.15 = (bf16[64,512]{1,0:T(8,128)(2,1)S(1)}, bf16[64,512]{1,0:T(8,128)(2,1)S(1)}, u32[]{:S(2)}, u32[]{:S(2)}) collective-permute-start(bf16[64,512]{1,0:T(8,128)(2,1)S(1)} %get-tuple-element.76.mark_ref), channel_id=1, source_target_pairs={{0,12},{2,14},{4,8},{6,10},{8,4},{10,6},{12,0},{14,2},{1,13},{3,15... | collective-permute-start | bytes 196616 | tf_op jit(solution)/shard_map/ppermute | solution.py:197
  41.9 4.7 %collective-permute-start.13 = (bf16[64,512]{1,0:T(8,128)(2,1)S(1)}, bf16[64,512]{1,0:T(8,128)(2,1)S(1)}, u32[]{:S(2)}, u32[]{:S(2)}) collective-permute-start(bf16[64,512]{1,0:T(8,128)(2,1)S(1)} %add_convert_fusion.2), channel_id=1, source_target_pairs={{0,4},{2,6},{4,0},{6,2},{8,12},{10,14},{12,8},{14,10},{1,5},{3,7},... | collective-permute-start | bytes 196616 | tf_op jit(solution)/shard_map/ppermute | solution.py:197
  45.2 3.6 %copy-start = (bf16[2,32,2048]{2,1,0:T(8,128)(2,1)S(1)}, bf16[2,32,2048]{2,1,0:T(8,128)(2,1)}, u32[]{:S(2)}) copy-start(bf16[2,32,2048]{2,1,0:T(8,128)(2,1)} %param.9) | copy-start | bytes 786436
  47.2 6.4 %collective-permute-start.16 = (bf16[64,2048]{1,0:T(8,128)(2,1)S(1)}, bf16[64,2048]{1,0:T(8,128)(2,1)S(1)}, u32[]{:S(2)}, u32[]{:S(2)}) collective-permute-start(bf16[64,2048]{1,0:T(8,128)(2,1)S(1)} %get-tuple-element.74), channel_id=1, source_target_pairs={{0,1},{1,0},{2,3},{3,2},{4,5},{5,4},{6,7},{7,6},{8,9},{9,8},{10,11... | collective-permute-start | bytes 786440 | tf_op jit(solution)/shard_map/ppermute | solution.py:188
